TPU v7x, 512 devices: a whole 4x8x8 slice. The times are simulated.
512 devices in a mesh: prow: 8 (over y), pcol: 64 (over x, z, core).
Axes of the slice: x: 4, y: 8, z: 8, core: 2. Of those that a mesh axis runs over, the one named last changes fastest.
Arguments:
- sigma_anc: float32 [6144, 6144], P('prow', 'pcol'), as said below
- panel_top: float32 [6144, 2048], P('prow', 'pcol'), may hold values from -0.3 to 0.3
- pivot_top: float32 [2048, 2048], P('prow', 'pcol'), as said below
- flags_top: int32 [192], replicated, may hold values from 0 to 1, as said below
- panel_kids: float32 [2, 2048, 1024], P(None, 'prow', 'pcol'), may hold values from -0.3 to 0.3
- pivot_kids: float32 [2, 1024, 1024], P(None, 'prow', 'pcol'), as said below
- flags_kids: int32 [2, 64], replicated, may hold values 0 or 1
Outputs:
- cross_top: float32 [2048, 6144], P('prow', 'pcol')
- sigma_top: float32 [2048, 2048], P('prow', 'pcol')
- cross_kids: float32 [2, 1024, 2048], P(None, 'prow', 'pcol')
- sigma_kids: float32 [2, 1024, 1024], P(None, 'prow', 'pcol')
Inputs may be any that keep to these rules, and one draw needn't show every extreme that they name: `sigma_anc`: exactly symmetric. `pivot_top`: exactly symmetric. `pivot_kids`: each matrix exactly symmetric. `flags_top`: in each aligned window of 24 consecutive entries at most 16 are 1, and some window has exactly 16.
All inputs are finite; a program needn't handle non-finite values.
Results may differ from a plain program's by a relative error of at most 0.000073.
Values sent between devices are 32-bit elements; how exact they have to be, the bound alone decides.
No kernel may reach another device: no remote copies, remote signals or barrier semaphores. Data moves between devices by JAX's collectives and lax.ppermute only.
A program may use at most 64 MiB of HBM per device.

v0:
```python
import jax
import jax.numpy as jnp
from jax import lax
from jax.sharding import PartitionSpec as P

BLK = 32


HIGH = lax.Precision.HIGHEST


def from_root(block, axis, source):
    block = jnp.where(lax.axis_index(axis) == source, block, jnp.zeros_like(block))
    return lax.psum(block, axis)


def block_keep(flags, first_row, count):
    row_ids = (first_row + jnp.arange(count, dtype=jnp.int32)) // BLK
    block_ids = jnp.arange(flags.shape[-1], dtype=jnp.int32)
    equal = row_ids[:, None] == block_ids[None, :]
    return jnp.sum(jnp.where(equal, flags[..., None, :], 0), axis=-1).astype(jnp.float32)


def finish_node(term_part, owned_rows, pivot_block, col_keep, owner_root):
    owned_all = from_root(owned_rows, "prow", owner_root)
    reduced = lax.psum_scatter(term_part, "prow", scatter_dimension=1, tiled=True)
    cross_block = -(reduced * col_keep[:, None, :])
    value = lax.dot_general(
        owned_all,
        reduced,
        (((1,), (2,)), ((0,), (0,))),
        precision=HIGH,
        preferred_element_type=jnp.float32,
    )
    summed = lax.psum_scatter(
        jnp.transpose(value, (1, 0, 2)), "pcol", scatter_dimension=0, tiled=True
    )
    return (cross_block, pivot_block + jnp.transpose(summed, (1, 2, 0)))


def per_device(sigma_anc, panel_top, pivot_top, flags_top, panel_kids, pivot_kids, flags_kids):
    prow_count = lax.axis_size("prow")
    pcol_count = lax.axis_size("pcol")
    prow_id = lax.axis_index("prow")
    pcol_id = lax.axis_index("pcol")
    anc_own = sigma_anc.shape[0]
    anc_col = sigma_anc.shape[1]
    owner_root = pcol_id * prow_count // pcol_count
    top_offset = jnp.clip(pcol_id * anc_col - prow_id * anc_own, 0, anc_own - anc_col)
    blocks_own = anc_own // BLK
    window = lax.dynamic_slice_in_dim(flags_top, prow_id * blocks_own, blocks_own)
    keep_own = jnp.repeat(window, BLK).astype(jnp.float32)
    masked_top = panel_top * keep_own[:, None]
    fragment = lax.all_gather(masked_top, "pcol", axis=1, tiled=True)
    product_part = lax.dot_general(
        fragment,
        sigma_anc,
        (((0,), (0,)), ((), ())),
        precision=HIGH,
        preferred_element_type=jnp.float32,
    )
    term_acc = product_part
    picked = lax.dynamic_slice_in_dim(fragment, top_offset, anc_col, 0)
    owned_acc = picked
    term_top = term_acc
    owned_top = owned_acc
    keep_cols_top = block_keep(flags_top, pcol_id * anc_col, anc_col)
    cross_top, sigma_stack = finish_node(
        term_top[None], owned_top[None], pivot_top[None], keep_cols_top[None], owner_root
    )
    sigma_block = sigma_stack[0]
    top_col = sigma_block.shape[1]
    kid_rows = panel_kids.shape[1]
    keep_kids = block_keep(flags_kids, prow_id * kid_rows, kid_rows)
    masked_kids = panel_kids * keep_kids[:, :, None]
    kid_offset = jnp.clip(pcol_id * top_col - prow_id * kid_rows, 0, kid_rows - top_col)
    fragment = lax.all_gather(masked_kids, "pcol", axis=2, tiled=True)
    product_part = lax.dot_general(
        fragment,
        sigma_block,
        (((1,), (0,)), ((), ())),
        precision=HIGH,
        preferred_element_type=jnp.float32,
    )
    term_acc = product_part
    picked = lax.dynamic_slice_in_dim(fragment, kid_offset, top_col, 1)
    owned_acc = picked
    keep_cols_kids = block_keep(flags_kids, pcol_id * top_col, top_col)
    cross_kids, sigma_kids = finish_node(
        term_acc, owned_acc, pivot_kids, keep_cols_kids, owner_root
    )
    return (cross_top[0], sigma_block, cross_kids, sigma_kids)


def solution(mesh):
    placed = (
        P("prow", "pcol"),
        P("prow", "pcol"),
        P("prow", "pcol"),
        P(),
        P(None, "prow", "pcol"),
        P(None, "prow", "pcol"),
        P(),
    )
    return jax.shard_map(
        per_device,
        mesh=mesh,
        in_specs=placed,
        out_specs=(
            P("prow", "pcol"),
            P("prow", "pcol"),
            P(None, "prow", "pcol"),
            P(None, "prow", "pcol"),
        ),
        check_vma=False,
    )
```

profile of v0, /device:TPU:1, one launch (start us, length us, event | category | flops | bytes accessed | tf_op | source)
XLA Modules:
  0.0 668.2 jit_solution(5752862587178104519)
XLA Ops:
  7.3 0.8 select_reduce_fusion
  8.1 1.4 broadcast_multiply_fusion.1
  9.5 0.8 dynamic-slice_convert_fusion
  10.3 0.1 convert_element_type.33
  10.4 1.5 broadcast_multiply_fusion
  12.1 89.2 %all-gather.5.cloned.1.call-done = f32[2,256,1024]{1,2,0:T(8,128)} async-done(((f32[2,256,16]{1,2,0:T(8,128)}), f32[2,256,1024]{1,2,0:T(8,128)}) %all-gather.5.cloned.1.call-update) | async-done | bytes 2097168 | tf_op jit(solution)/shard_map/all_gather | solution.py:77
  101.2 2.9 dynamic-slice_select_fusion
  104.2 85.4 %all-gather.3.cloned.1.call-done = f32[768,2048]{0,1:T(8,128)} async-done(((f32[768,32]{0,1:T(8,128)}), f32[768,2048]{0,1:T(8,128)}) %all-gather.3.cloned.1.call-update) | async-done | bytes 6291472 | tf_op jit(solution)/shard_map/all_gather | solution.py:54
  189.5 2.9 dynamic-slice_select_fusion.1
  192.5 9.9 %convolution_bitcast_fusion.1 = f32[1,2048,96]{1,2,0:T(8,128)} fusion(f32[768,2048]{0,1:T(8,128)} %all-gather.3.cloned.1.call-done, f32[768,96]{0,1:T(8,128)S(1)} %copy-done), kind=kOutput, calls=%fused_computation.1 | convolution fusion | flops 1811939328 | bytes 7372800 | tf_op jit(solution)/shard_map/dot_general | solution.py:55
  202.5 70.3 %all-reduce.3.cloned.1.call-done = (f32[96,2048]{0,1:T(8,128)}, f32[2,32,1024]{1,2,0:T(8,128)}) async-done(((f32[96,2048]{0,1:T(8,128)}, f32[2,32,1024]{1,2,0:T(8,128)}), (f32[96,2048]{0,1:T(8,128)}, f32[2,32,1024]{1,2,0:T(8,128)})) %all-reduce.3.cloned.1.call-update) | async-done | bytes 1048592 | tf_op jit(solution)/shard_map/psum | solution.py:14
  272.8 40.4 %reduce-scatter.5.cloned.1.call-done = f32[1,256,96]{1,2,0:T(8,128)} async-done(((f32[1,2048,96]{1,2,0:T(8,128)}), f32[1,256,96]{1,2,0:T(8,128)}) %reduce-scatter.5.cloned.1.call-update) | async-done | bytes 98320 | tf_op jit(solution)/shard_map/reduce_scatter | solution.py:26
  313.3 4.5 convolution_bitcast_fusion
  317.8 148.9 %reduce-scatter.7.cloned.1.call-done = f32[32,1,256]{2,0,1:T(8,128)} async-done(((f32[2048,1,256]{2,0,1:T(8,128)}), f32[32,1,256]{2,0,1:T(8,128)}) %reduce-scatter.7.cloned.1.call-update) | async-done | bytes 32784 | tf_op jit(solution)/shard_map/reduce_scatter | solution.py:35
  466.8 3.5 fusion.1
  470.3 36.9 %reduce-scatter.9.cloned.1.call-done = f32[2,128,32]{1,2,0:T(8,128)} async-done(((f32[2,1024,32]{1,2,0:T(8,128)}), f32[2,128,32]{1,2,0:T(8,128)}) %reduce-scatter.9.cloned.1.call-update) | async-done | bytes 32784 | tf_op jit(solution)/shard_map/reduce_scatter | solution.py:26
  507.2 2.8 convolution_bitcast_fusion.2
  510.1 0.2 select_reduce_fusion.1
  510.4 0.1 select_reduce_fusion.2
  510.5 0.7 negate_bitcast_fusion
  511.2 0.6 fusion.3
  511.8 0.7 multiply_negate_fusion
  512.5 147.5 %reduce-scatter.11.cloned.1.call-done = f32[16,2,128]{2,0,1:T(8,128)} async-done(((f32[1024,2,128]{2,0,1:T(8,128)}), f32[16,2,128]{2,0,1:T(8,128)}) %reduce-scatter.11.cloned.1.call-update) | async-done | bytes 16400 | tf_op jit(solution)/shard_map/reduce_scatter | solution.py:35
  660.1 1.3 bitcast_add_fusion.1
  (43 shorter events, 0.7 us)
Async XLA Ops:
  7.2 185.4 %copy-start = (f32[768,96]{0,1:T(8,128)S(1)}, f32[768,96]{0,1:T(8,128)}, u32[]{:S(2)}) copy-start(f32[768,96]{0,1:T(8,128)} %param.7) | copy-start | bytes 884740
  7.2 94.1 %all-gather.5.cloned.1.call-start = ((), (), s32[]{:S(2)}) async-start(), calls=%async_computation.7 | async-start | bytes 2129920 | tf_op jit(solution)/shard_map/all_gather | solution.py:77
  9.5 180.1 %all-gather.3.cloned.1.call-start = ((), (), s32[]{:S(2)}) async-start(), calls=%async_computation.4 | async-start | bytes 6389760 | tf_op jit(solution)/shard_map/all_gather | solution.py:54
  12.0 260.8 %all-reduce.3.cloned.1.call-start = ((), (), s32[]{:S(2)}) async-start(), calls=%async_computation.10 | async-start | bytes 4194304 | tf_op jit(solution)/shard_map/psum | solution.py:14
  192.5 120.8 %reduce-scatter.5.cloned.1.call-start = ((), (), s32[]{:S(2)}) async-start(), calls=%async_computation.5 | async-start | bytes 884736 | tf_op jit(solution)/shard_map/reduce_scatter | solution.py:26
  202.5 264.3 %reduce-scatter.7.cloned.1.call-start = ((), (), s32[]{:S(2)}) async-start(), calls=%async_computation.6 | async-start | bytes 2129920 | tf_op jit(solution)/shard_map/reduce_scatter | solution.py:35
  313.3 153.5 %copy-start.1 = (f32[2,256,1024]{1,2,0:T(8,128)S(1)}, f32[2,256,1024]{1,2,0:T(8,128)}, u32[]{:S(2)}) copy-start(f32[2,256,1024]{1,2,0:T(8,128)} %all-gather.5.cloned.1.call-done) | copy-start | bytes 6291460
  313.3 153.5 %copy-start.4 = (f32[256,32]{0,1:T(8,128)S(1)}, f32[256,32]{0,1:T(8,128)}, u32[]{:S(2)}) copy-start(f32[256,32]{0,1:T(8,128)} %param.9) | copy-start | bytes 98308
  317.8 189.5 %copy-start.2 = (f32[2,32,1024]{1,2,0:T(8,128)S(1)}, f32[2,32,1024]{1,2,0:T(8,128)}, u32[]{:S(2)}) copy-start(f32[2,32,1024]{1,2,0:T(8,128)} %get-tuple-element.5) | copy-start | bytes 786436
  317.8 189.4 %reduce-scatter.9.cloned.1.call-start = ((), (), s32[]{:S(2)}) async-start(), calls=%async_computation.8 | async-start | bytes 294912 | tf_op jit(solution)/shard_map/reduce_scatter | solution.py:26
  470.2 39.8 %copy-start.9 = (s32[192]{0:T(256)S(1)}, s32[192]{0:T(256)}, u32[]{:S(2)}) copy-start(s32[192]{0:T(256)} %param.10) | copy-start | bytes 2308
  470.2 40.1 %copy-start.8 = (s32[2,64]{1,0:T(2,128)S(1)}, s32[2,64]{1,0:T(2,128)}, u32[]{:S(2)}) copy-start(s32[2,64]{1,0:T(2,128)} %param.13) | copy-start | bytes 1540
  470.2 40.2 %copy-start.3 = (f32[1,256,96]{1,2,0:T(8,128)S(1)}, f32[1,256,96]{1,2,0:T(8,128)}, u32[]{:S(2)}) copy-start(f32[1,256,96]{1,2,0:T(8,128)} %reduce-scatter.5.cloned.1.call-done) | copy-start | bytes 294916
  470.3 41.0 %copy-start.5 = (f32[32,1,256]{2,0,1:T(8,128)S(1)}, f32[32,1,256]{2,0,1:T(8,128)}, u32[]{:S(2)}) copy-start(f32[32,1,256]{2,0,1:T(8,128)} %reduce-scatter.7.cloned.1.call-done) | copy-start | bytes 98308
  470.3 189.8 %copy-start.7 = (f32[2,128,16]{1,2,0:T(8,128)S(1)}, f32[2,128,16]{1,2,0:T(8,128)}, u32[]{:S(2)}) copy-start(f32[2,128,16]{1,2,0:T(8,128)} %param.12) | copy-start | bytes 49156
  470.3 189.8 %reduce-scatter.11.cloned.1.call-start = ((), (), s32[]{:S(2)}) async-start(), calls=%async_computation.9 | async-start | bytes 1064960 | tf_op jit(solution)/shard_map/reduce_scatter | solution.py:35
  507.2 4.6 copy-start.6
Sparse Core Ops, SparseCore 0:
  12.0 89.2 all-gather.4
  105.1 84.3 all-gather.2
  192.6 80.1 all-reduce.2
  275.5 37.7 reduce-scatter.4
  318.4 148.2 reduce-scatter.6
  470.4 36.7 reduce-scatter.8
  512.4 147.5 reduce-scatter.10
where the time goes:
time: 673 us; the launch traced here: 668 us
  waiting for transfers between devices  619 us (92%)
  matrix products  20.7 us (3%)
  between operations  14.3 us (2%)
  other arithmetic  14.1 us (2%)
    reduce_scatter x2, waiting for transfers between devices, finish_node(): lax.psum_scatter(jnp.transpose(value, (1, 0, 2)), 'pcol', scatter_dimensi...  296 us
    all_gather x1, waiting for transfers between devices, per_device(): fragment = lax.all_gather(masked_kids, 'pcol', axis=2, tiled=True)  89.2 us
    all_gather x1, waiting for transfers between devices, per_device(): fragment = lax.all_gather(masked_top, 'pcol', axis=1, tiled=True)  85.4 us
    reduce_scatter x2, waiting for transfers between devices, finish_node(): lax.psum_scatter(term_part, 'prow', scatter_dimension=1, tiled=True)  77.3 us
    psum x1, waiting for transfers between devices, from_root(): return lax.psum(block, axis)  70.3 us
  transfers between devices with their start and end apart: 7, of which 7 were waited for; matrix products, arithmetic and copies ran while one was open for 3% of the time, Pallas kernels for 0%

commit v1 on v0

v1 whole, which is shorter than its diff:
```python
import jax
import jax.numpy as jnp
from jax import lax
from jax.sharding import Mesh
from jax.sharding import PartitionSpec as P

BLK = 32
LIVE = 16
HIGH = lax.Precision.HIGH
WIN = ("x", "h")
SUB = ("q", "c")


def dot_nt(a, b):
    return lax.dot_general(
        a, b, (((1,), (1,)), ((), ())), precision=HIGH, preferred_element_type=jnp.float32
    )


def pieces(value):
    high = lax.reduce_precision(value, 8, 7)
    rest = value - high
    mid = lax.reduce_precision(rest, 8, 7)
    return [part.astype(jnp.bfloat16) for part in (high, mid, rest - mid)]


def select_exact(value, choice):
    rows = value.shape[0]
    stacked = jnp.concatenate(pieces(value), axis=0)
    picked = lax.dot_general(
        stacked, choice, (((1,), (0,)), ((), ())), preferred_element_type=jnp.float32
    )
    return picked[:rows] + (picked[rows : 2 * rows] + picked[2 * rows :])


def slot_choice(window, block_ids, count):
    order = jnp.arange(window.shape[0])
    rank = jnp.sum(jnp.where(order[None, :] < order[:, None], window[None, :], 0), axis=1)
    slot = jnp.where(window == 1, rank, -1)
    slot_of = jnp.sum(
        jnp.where(block_ids[:, None] == jnp.arange(window.shape[0])[None, :], slot[None, :], 0), axis=1
    )
    slot_of = jnp.broadcast_to(slot_of[:, None], (block_ids.shape[0], BLK)).reshape(-1)
    place = slot_of * BLK + jnp.arange(block_ids.shape[0] * BLK, dtype=jnp.int32) % BLK
    place = jnp.where(slot_of >= 0, place, -1)
    return (place[:, None] == jnp.arange(count, dtype=jnp.int32)[None, :]).astype(jnp.bfloat16)


def swap(value, axis):
    return lax.ppermute(value, axis, [(0, 1), (1, 0)])


def sum_over(parts, axis):
    return jnp.sum(lax.all_to_all(parts, axis, 0, 0, tiled=True), axis=0)


def turn(value, count):
    places = [(i, j) for i in range(count) for j in range(count)]
    for goes in (lambda i, j: ((i + j) % count, j), lambda i, j: (i, (i - j) % count)):
        order = [(i * count + j, goes(i, j)[0] * count + goes(i, j)[1]) for i, j in places]
        value = lax.ppermute(value, ("y",) + WIN, order)
    return value


def in_order(parts, first):
    twice = jnp.concatenate([parts, parts], axis=0)
    return lax.dynamic_slice_in_dim(twice, first, parts.shape[0], 0)


def spread(value, axis):
    copies = jnp.broadcast_to(value[None], (lax.axis_size(axis),) + value.shape)
    return lax.all_to_all(copies, axis, 0, 0, tiled=True)


def gather_sub(rows):
    lines = spread(rows, "q")
    both = lax.all_gather(lines, "c", axis=1)
    return both.reshape((-1,) + rows.shape)


def per_device(sigma_anc, panel_top, pivot_top, flags_top, panel_kids, pivot_kids, flags_kids):
    ny, nx, nh = lax.axis_size("y"), lax.axis_size("x"), lax.axis_size("h")
    nq = lax.axis_size("q")
    y_id, q_id, c_id, h_id = (lax.axis_index(a) for a in ("y", "q", "c", "h"))
    win_id = lax.axis_index("x") * nh + h_id
    sub_id = q_id * 2 + c_id
    anc_own, anc_col = sigma_anc.shape
    per_win = anc_own // BLK
    per_col = anc_col // BLK
    live = LIVE * BLK
    top_col = panel_top.shape[1]
    kid_own = panel_kids.shape[1]
    kid_col = panel_kids.shape[2]

    row_window = lax.dynamic_slice_in_dim(flags_top, y_id * per_win, per_win)
    col_window = lax.dynamic_slice_in_dim(flags_top, win_id * per_win, per_win)
    row_choice = slot_choice(row_window, jnp.arange(per_win), live)
    group = jnp.arange(nq * per_col) // per_col
    within = jnp.arange(nq * per_col) % per_col
    near_choice = slot_choice(col_window, (group * 2 + c_id) * per_col + within, live)
    far_choice = slot_choice(col_window, (group * 2 + 1 - c_id) * per_col + within, live)
    own_choice = slot_choice(col_window, sub_id * per_col + jnp.arange(per_col), live)

    packed = select_exact(jnp.concatenate([sigma_anc.T, panel_top.T], axis=0), row_choice)
    field = packed[:anc_col]
    top_rows = packed[anc_col:]
    kid_blocks = kid_own // BLK
    kid_flags = lax.dynamic_slice_in_dim(flags_kids, y_id * kid_blocks, kid_blocks, 1)
    keep_rows = jnp.repeat(kid_flags, BLK, axis=1).astype(jnp.float32)
    kids = jnp.transpose(panel_kids, (0, 2, 1)) * keep_rows[:, None, :]
    panel = jnp.concatenate([top_rows, kids.reshape(2 * kid_col, kid_own)], axis=1)

    turned = turn(panel, ny)
    other = swap(panel, "h")
    near = lax.all_gather(field, "q", axis=0).reshape(nq * anc_col, live)
    near, other, turned = lax.optimization_barrier((near, other, turned))
    far = swap(near, "c")
    pair = jnp.stack([jnp.where(h_id == 0, panel, other), jnp.where(h_id == 0, other, panel)])
    turned = spread(turned, "y").reshape(ny * top_col, live + kid_own)
    wide = spread(pair, "x").reshape(ny * top_col, live + kid_own)

    top_wide = wide[:, :live]
    zed = select_exact(dot_nt(top_wide, near), near_choice) + select_exact(
        dot_nt(top_wide, far), far_choice
    )
    zed, turned = lax.optimization_barrier((zed, turned))
    zed = sum_over(zed.reshape(ny, top_col, live), "y")
    zed = gather_sub(zed).reshape(-1, live)
    cross_top = -lax.dot_general(
        own_choice, jnp.concatenate(pieces(zed), axis=0), (((1,), (1,)), ((), ())),
        preferred_element_type=jnp.float32,
    ).reshape(anc_col, 3, -1).sum(axis=1)

    part = dot_nt(turned[:, :live], zed)
    sigma_top = pivot_top.T + sum_over(
        in_order(part.reshape(nx * nh, top_col, -1), win_id), WIN
    )

    block = gather_sub(sigma_top).reshape(-1, kid_own)
    part = dot_nt(wide[:, live:], block)
    zed = sum_over(part.reshape(ny, 2 * kid_col, -1), "y")
    zed = gather_sub(zed.reshape(2, kid_col, -1))
    zed = jnp.transpose(zed, (1, 0, 2, 3)).reshape(2, -1, kid_own)
    col_flags = lax.dynamic_slice_in_dim(flags_kids, win_id * kid_blocks + sub_id, 1, 1)
    cross_kids = lax.dynamic_slice_in_dim(zed, sub_id * top_col, top_col, 2)
    cross_kids = -(cross_kids * col_flags.astype(jnp.float32)[:, :, None])

    turned_kids = turned[:, live:].reshape(nx * nh, 2, kid_col, kid_own)
    part = jnp.stack(
        [dot_nt(turned_kids[:, k].reshape(-1, kid_own), zed[k]) for k in range(2)]
    )
    part = jnp.transpose(part.reshape(2, nx * nh, kid_col, -1), (1, 0, 2, 3))
    sigma_kids = jnp.transpose(pivot_kids, (0, 2, 1)) + sum_over(in_order(part, win_id), WIN)
    return (
        cross_top.T,
        sigma_top.T,
        cross_kids,
        jnp.transpose(sigma_kids, (0, 2, 1)),
    )


def solution(mesh):
    fine = Mesh(mesh.devices.reshape(8, 4, 2, 4, 2), ("y", "x", "h", "q", "c"))
    cols = ("x", "h", "q", "c")
    flat = P("y", cols)
    kids = P(None, "y", cols)
    return jax.shard_map(
        per_device,
        mesh=fine,
        in_specs=(flat, flat, flat, P(), kids, kids, P()),
        out_specs=(flat, flat, kids, kids),
        check_vma=False,
    )
```

time: 673 us -> 200 us (0.30)
  waiting for transfers between devices: 619 us -> 59 us
  starting transfers between devices: 0.29 us -> 68.7 us
  blocking collectives: 0 us -> 49.4 us
  matrix products: 20.7 us -> 6.59 us
  between operations: 14.3 us -> 1.08 us
  other arithmetic: 14.1 us -> 5.85 us
  local copies, waits for them, and re-layouts: 0.19 us -> 8.43 us
    reduce_scatter x4 -> x0, waiting for transfers between devices: 374 us -> none  [the longest x2 296 us: finish_node(): lax.psum_scatter(jnp.transpose(value, (1, 0, 2)), 'pcol', scatter_dimensi...]
    all_gather x2 -> x0, waiting for transfers between devices: 175 us -> none  [the longest x1 89.2 us: per_device(): fragment = lax.all_gather(masked_kids, 'pcol', axis=2, tiled=True)]
    psum x1 -> x0, waiting for transfers between devices: 70.3 us -> none  [from_root(): return lax.psum(block, axis)]
    all_to_all x0 -> x8, waiting for transfers between devices: none -> 58.9 us  [the longest x3 29.6 us: sum_over(): return jnp.sum(lax.all_to_all(parts, axis, 0, 0, tiled=True), axis=0)]
    all_to_all x0 -> x8, starting transfers between devices: none -> 46.8 us  [the longest x5 36.6 us: spread(): return lax.all_to_all(copies, axis, 0, 0, tiled=True)]
    all_gather x0 -> x4, blocking collectives: none -> 34.6 us  [the longest x1 18.1 us: per_device(): near = lax.all_gather(field, 'q', axis=0).reshape(nq * anc_col, live)]
    ppermute x0 -> x4, starting transfers between devices: none -> 22 us  [the longest x2 20.6 us: swap(): return lax.ppermute(value, axis, [(0, 1), (1, 0)])]
    all_to_all x0 -> x1, blocking collectives: none -> 14.8 us  [sum_over(): return jnp.sum(lax.all_to_all(parts, axis, 0, 0, tiled=True), axis=0)]
  transfers between devices with their start and end apart: 7 -> 12, of which waited for: 7 -> 8; matrix products, arithmetic and copies ran while one was open for 3% -> 5% of each run, Pallas kernels for 0% -> 0%
where the time goes in v1:
time: 200 us; the launch traced here: 199 us
  starting transfers between devices  68.7 us (34%)
  waiting for transfers between devices  59 us (30%)
  blocking collectives  49.4 us (25%)
  local copies, waits for them, and re-layouts  8.43 us (4%)
  matrix products  6.59 us (3%)
  other arithmetic  5.85 us (3%)
    all_to_all x5, starting transfers between devices, spread(): return lax.all_to_all(copies, axis, 0, 0, tiled=True)  36.6 us
    all_to_all x3, waiting for transfers between devices, sum_over(): return jnp.sum(lax.all_to_all(parts, axis, 0, 0, tiled=True), axis=0)  29.6 us
    all_to_all x5, waiting for transfers between devices, spread(): return lax.all_to_all(copies, axis, 0, 0, tiled=True)  29.3 us
    ppermute x2, starting transfers between devices, swap(): return lax.ppermute(value, axis, [(0, 1), (1, 0)])  20.6 us
    all_gather x1, blocking collectives, per_device(): near = lax.all_gather(field, 'q', axis=0).reshape(nq * anc_col, live)  18.1 us
    all_gather x3, blocking collectives, gather_sub(): both = lax.all_gather(lines, 'c', axis=1)  16.5 us
    all_to_all x1, blocking collectives, sum_over(): return jnp.sum(lax.all_to_all(parts, axis, 0, 0, tiled=True), axis=0)  14.8 us
    all_to_all x3, starting transfers between devices, sum_over(): return jnp.sum(lax.all_to_all(parts, axis, 0, 0, tiled=True), axis=0)  10.2 us
  transfers between devices with their start and end apart: 12, of which 8 were waited for; matrix products, arithmetic and copies ran while one was open for 5% of the time, Pallas kernels for 0%

profile of v1, /device:TPU:1, one launch (start us, length us, event | category | flops | bytes accessed | tf_op | source)
XLA Modules:
  0.0 199.0 jit_solution(1251000068456054295)
XLA Ops:
  2.1 1.1 reduce-precision_convert_fusion.7
  5.4 14.0 %collective-permute-start = (f32[32,768]{1,0:T(8,128)S(1)}, f32[32,768]{1,0:T(8,128)S(1)}, u32[]{:S(2)}, u32[]{:S(2)}) collective-permute-start(f32[32,768]{1,0:T(8,128)S(1)} %pad_maximum_fusion.2), channel_id=1, source_target_pairs={{0,8},{8,0},{1,9},{9,1},{2,10},{10,2},{3,11},{11,3},{4,12},{12,4},... | collective-permute-start | bytes 294920 | tf_op jit(solution)/shard_map/ppermute | solution.py:50
  19.4 18.1 %all-gather = f32[384,512]{1,0:T(8,128)S(1)} all-gather(f32[96,512]{1,0:T(8,128)S(1)} %slice.82), channel_id=2, replica_groups=mesh['y'=8,'x'=4,'h'=2,'q'=4,'c'=2] {'q'}, dimensions={0}, use_global_device_ids=true | all-gather | bytes 983040 | tf_op jit(solution)/shard_map/all_gather | solution.py:115
  39.6 11.8 %all-to-all-start = ((f32[4,2,32,768]{3,2,1,0:T(8,128)}), f32[4,2,32,768]{3,2,1,0:T(8,128)S(1)}, u32[]{:S(2)}, u32[]{:S(2)}) async-start(f32[4,2,32,768]{3,2,1,0:T(8,128)} %broadcast_in_dim.194), calls=%async_computation | async-start | bytes 1572864 | tf_op jit(solution)/shard_map/all_to_all | solution.py:72
  51.4 6.6 %collective-permute-start.3 = (f32[384,512]{1,0:T(8,128)S(1)}, f32[384,512]{1,0:T(8,128)}, u32[]{:S(2)}, u32[]{:S(2)}) collective-permute-start(f32[384,512]{1,0:T(8,128)S(1)} %all-gather), channel_id=1, source_target_pairs={{0,1},{1,0},{2,3},{3,2},{4,5},{5,4},{6,7},{7,6},{8,9},{9,8},{10,11... | collective-permute-start | bytes 2359304 | tf_op jit(solution)/shard_map/ppermute | solution.py:50
  60.7 9.5 %all-to-all-start.1 = ((f32[8,32,768]{2,1,0:T(8,128)}), f32[8,32,768]{2,1,0:T(8,128)S(1)}, u32[]{:S(2)}, u32[]{:S(2)}) async-start(f32[8,32,768]{2,1,0:T(8,128)} %broadcast_in_dim.202), calls=%async_computation.1 | async-start | bytes 1572864 | tf_op jit(solution)/shard_map/all_to_all | solution.py:72
  71.5 1.7 reduce-precision_convert_fusion.3
  74.3 13.8 %all-to-all-done.1 = f32[8,32,768]{2,1,0:T(8,128)S(1)} async-done(((f32[8,32,768]{2,1,0:T(8,128)}), f32[8,32,768]{2,1,0:T(8,128)S(1)}, u32[]{:S(2)}, u32[]{:S(2)}) %all-to-all-start.1) | async-done | bytes 786464 | tf_op jit(solution)/shard_map/all_to_all | solution.py:72
  88.1 14.8 %all_to_all.45 = f32[8,32,512]{2,1,0:T(8,128)S(1)} all-to-all(f32[8,32,512]{2,1,0:T(8,128)S(1)} %bitcast.78), channel_id=1, replica_groups=mesh['y'=8,'x'=4,'h'=2,'q'=4,'c'=2] {'y'}, dimensions={0} | all-to-all | bytes 1048576 | tf_op jit(solution)/shard_map/all_to_all | solution.py:54
  103.7 6.9 %all-to-all-start.3 = ((f32[4,32,512]{2,1,0:T(8,128)}), f32[4,32,512]{2,1,0:T(8,128)S(1)}, u32[]{:S(2)}, u32[]{:S(2)}) async-start(f32[4,32,512]{2,1,0:T(8,128)} %broadcast_in_dim.203), calls=%async_computation.3 | async-start | bytes 524288 | tf_op jit(solution)/shard_map/all_to_all | solution.py:72
  110.7 5.6 %all-to-all-done.3 = f32[4,32,512]{2,1,0:T(8,128)S(1)} async-done(((f32[4,32,512]{2,1,0:T(8,128)}), f32[4,32,512]{2,1,0:T(8,128)S(1)}, u32[]{:S(2)}, u32[]{:S(2)}) %all-to-all-start.3) | async-done | bytes 262176 | tf_op jit(solution)/shard_map/all_to_all | solution.py:72
  116.2 8.6 %all-gather.1 = f32[4,64,512]{2,1,0:T(8,128)S(1)} all-gather(f32[4,32,512]{2,1,0:T(8,128)S(1)} %all-to-all-done.3), channel_id=3, replica_groups=mesh['y'=8,'x'=4,'h'=2,'q'=4,'c'=2] {'c'}, dimensions={1}, use_global_device_ids=true | all-gather | bytes 786432 | tf_op jit(solution)/shard_map/all_gather | solution.py:77
  126.0 3.4 %all-to-all-start.4 = ((f32[8,32,256]{2,1,0:T(8,128)}), f32[8,32,256]{2,1,0:T(8,128)S(1)}, u32[]{:S(2)}, u32[]{:S(2)}) async-start(f32[8,32,256]{2,1,0:T(8,128)} %fusion.38), calls=%async_computation.4 | async-start | bytes 524288 | tf_op jit(solution)/shard_map/all_to_all | solution.py:54
  130.1 10.4 %all-to-all-done.4 = f32[8,32,256]{2,1,0:T(8,128)S(1)} async-done(((f32[8,32,256]{2,1,0:T(8,128)}), f32[8,32,256]{2,1,0:T(8,128)S(1)}, u32[]{:S(2)}, u32[]{:S(2)}) %all-to-all-start.4) | async-done | bytes 262176 | tf_op jit(solution)/shard_map/all_to_all | solution.py:54
  141.1 5.1 %all-to-all-start.5 = ((f32[4,32,256]{2,1,0:T(8,128)}), f32[4,32,256]{2,1,0:T(8,128)S(1)}, u32[]{:S(2)}, u32[]{:S(2)}) async-start(f32[4,32,256]{2,1,0:T(8,128)} %broadcast_in_dim.204), calls=%async_computation.5 | async-start | bytes 262144 | tf_op jit(solution)/shard_map/all_to_all | solution.py:72
  146.3 4.7 %all-to-all-done.5 = f32[4,32,256]{2,1,0:T(8,128)S(1)} async-done(((f32[4,32,256]{2,1,0:T(8,128)}), f32[4,32,256]{2,1,0:T(8,128)S(1)}, u32[]{:S(2)}, u32[]{:S(2)}) %all-to-all-start.5) | async-done | bytes 131104 | tf_op jit(solution)/shard_map/all_to_all | solution.py:72
  151.0 4.2 %all-gather.2 = f32[4,64,256]{2,1,0:T(8,128)S(1)} all-gather(f32[4,32,256]{2,1,0:T(8,128)S(1)} %all-to-all-done.5), channel_id=4, replica_groups=mesh['y'=8,'x'=4,'h'=2,'q'=4,'c'=2] {'c'}, dimensions={1}, use_global_device_ids=true | all-gather | bytes 393216 | tf_op jit(solution)/shard_map/all_gather | solution.py:77
  156.3 3.4 %all-to-all-start.6 = ((f32[8,32,256]{2,1,0:T(8,128)}), f32[8,32,256]{2,1,0:T(8,128)S(1)}, u32[]{:S(2)}, u32[]{:S(2)}) async-start(f32[8,32,256]{2,1,0:T(8,128)} %fusion.63), calls=%async_computation.6 | async-start | bytes 524288 | tf_op jit(solution)/shard_map/all_to_all | solution.py:54
  160.6 11.4 %all-to-all-done.6 = f32[8,32,256]{2,1,0:T(8,128)S(1)} async-done(((f32[8,32,256]{2,1,0:T(8,128)}), f32[8,32,256]{2,1,0:T(8,128)S(1)}, u32[]{:S(2)}, u32[]{:S(2)}) %all-to-all-start.6) | async-done | bytes 262176 | tf_op jit(solution)/shard_map/all_to_all | solution.py:54
  172.6 3.3 %all-to-all-start.7 = ((f32[4,2,16,256]{3,2,1,0:T(8,128)}), f32[4,2,16,256]{3,2,1,0:T(8,128)S(1)}, u32[]{:S(2)}, u32[]{:S(2)}) async-start(f32[4,2,16,256]{3,2,1,0:T(8,128)} %broadcast_in_dim.206), calls=%async_computation.7 | async-start | bytes 262144 | tf_op jit(solution)/shard_map/all_to_all | solution.py:72
  176.6 4.1 %all-to-all-done.7 = f32[4,2,16,256]{3,2,1,0:T(8,128)S(1)} async-done(((f32[4,2,16,256]{3,2,1,0:T(8,128)}), f32[4,2,16,256]{3,2,1,0:T(8,128)S(1)}, u32[]{:S(2)}, u32[]{:S(2)}) %all-to-all-start.7) | async-done | bytes 131104 | tf_op jit(solution)/shard_map/all_to_all | solution.py:72
  180.7 3.7 %all-gather.3 = f32[4,4,16,256]{3,2,1,0:T(8,128)S(1)} all-gather(f32[4,2,16,256]{3,2,1,0:T(8,128)S(1)} %all-to-all-done.7), channel_id=5, replica_groups=mesh['y'=8,'x'=4,'h'=2,'q'=4,'c'=2] {'c'}, dimensions={1}, use_global_device_ids=true | all-gather | bytes 393216 | tf_op jit(solution)/shard_map/all_gather | solution.py:77
  185.6 3.4 %all-to-all-start.8 = ((f32[8,2,16,128]{3,2,1,0:T(8,128)}), f32[8,2,16,128]{3,2,1,0:T(8,128)S(1)}, u32[]{:S(2)}, u32[]{:S(2)}) async-start(f32[8,2,16,128]{3,2,1,0:T(8,128)} %copy.24), calls=%async_computation.8 | async-start | bytes 262144 | tf_op jit(solution)/shard_map/all_to_all | solution.py:54
  190.5 7.9 %all-to-all-done.8 = f32[8,2,16,128]{3,2,1,0:T(8,128)S(1)} async-done(((f32[8,2,16,128]{3,2,1,0:T(8,128)}), f32[8,2,16,128]{3,2,1,0:T(8,128)S(1)}, u32[]{:S(2)}, u32[]{:S(2)}) %all-to-all-start.8) | async-done | bytes 131104 | tf_op jit(solution)/shard_map/all_to_all | solution.py:54
  (101 shorter events, 20.4 us)
Async XLA Ops:
  3.7 0.7 copy-start.3
  3.8 0.9 copy-start.1
  4.7 33.2 %collective-permute-start.1 = (f32[32,768]{1,0:T(8,128)S(1)}, f32[32,768]{1,0:T(8,128)S(1)}, u32[]{:S(2)}, u32[]{:S(2)}) collective-permute-start(f32[32,768]{1,0:T(8,128)S(1)} %pad_maximum_fusion.2), channel_id=1, source_target_pairs={{0,0},{8,72},{16,144},{24,216},{32,288},{40,360},{48,432},{56,504}... | collective-permute-start | bytes 294920 | tf_op jit(solution)/shard_map/ppermute | solution.py:61
  5.4 33.2 %collective-permute-start = (f32[32,768]{1,0:T(8,128)S(1)}, f32[32,768]{1,0:T(8,128)S(1)}, u32[]{:S(2)}, u32[]{:S(2)}) collective-permute-start(f32[32,768]{1,0:T(8,128)S(1)} %pad_maximum_fusion.2), channel_id=1, source_target_pairs={{0,8},{8,0},{1,9},{9,1},{2,10},{10,2},{3,11},{11,3},{4,12},{12,4},... | collective-permute-start | bytes 294920 | tf_op jit(solution)/shard_map/ppermute | solution.py:50
  37.9 0.7 collective-permute-start.2
  39.6 20.1 %all-to-all-start = ((f32[4,2,32,768]{3,2,1,0:T(8,128)}), f32[4,2,32,768]{3,2,1,0:T(8,128)S(1)}, u32[]{:S(2)}, u32[]{:S(2)}) async-start(f32[4,2,32,768]{3,2,1,0:T(8,128)} %broadcast_in_dim.194), calls=%async_computation | async-start | bytes 1572864 | tf_op jit(solution)/shard_map/all_to_all | solution.py:72
  51.4 20.1 %collective-permute-start.3 = (f32[384,512]{1,0:T(8,128)S(1)}, f32[384,512]{1,0:T(8,128)}, u32[]{:S(2)}, u32[]{:S(2)}) collective-permute-start(f32[384,512]{1,0:T(8,128)S(1)} %all-gather), channel_id=1, source_target_pairs={{0,1},{1,0},{2,3},{3,2},{4,5},{5,4},{6,7},{7,6},{8,9},{9,8},{10,11... | collective-permute-start | bytes 2359304 | tf_op jit(solution)/shard_map/ppermute | solution.py:50
  60.7 27.4 %all-to-all-start.1 = ((f32[8,32,768]{2,1,0:T(8,128)}), f32[8,32,768]{2,1,0:T(8,128)S(1)}, u32[]{:S(2)}, u32[]{:S(2)}) async-start(f32[8,32,768]{2,1,0:T(8,128)} %broadcast_in_dim.202), calls=%async_computation.1 | async-start | bytes 1572864 | tf_op jit(solution)/shard_map/all_to_all | solution.py:72
  103.7 12.5 %all-to-all-start.3 = ((f32[4,32,512]{2,1,0:T(8,128)}), f32[4,32,512]{2,1,0:T(8,128)S(1)}, u32[]{:S(2)}, u32[]{:S(2)}) async-start(f32[4,32,512]{2,1,0:T(8,128)} %broadcast_in_dim.203), calls=%async_computation.3 | async-start | bytes 524288 | tf_op jit(solution)/shard_map/all_to_all | solution.py:72
  124.8 15.7 %copy-start = (f32[256,32]{0,1:T(8,128)S(1)}, f32[256,32]{0,1:T(8,128)}, u32[]{:S(2)}) copy-start(f32[256,32]{0,1:T(8,128)} %param.9) | copy-start | bytes 98308
  126.0 14.5 %all-to-all-start.4 = ((f32[8,32,256]{2,1,0:T(8,128)}), f32[8,32,256]{2,1,0:T(8,128)S(1)}, u32[]{:S(2)}, u32[]{:S(2)}) async-start(f32[8,32,256]{2,1,0:T(8,128)} %fusion.38), calls=%async_computation.4 | async-start | bytes 524288 | tf_op jit(solution)/shard_map/all_to_all | solution.py:54
  141.1 9.9 %all-to-all-start.5 = ((f32[4,32,256]{2,1,0:T(8,128)}), f32[4,32,256]{2,1,0:T(8,128)S(1)}, u32[]{:S(2)}, u32[]{:S(2)}) async-start(f32[4,32,256]{2,1,0:T(8,128)} %broadcast_in_dim.204), calls=%async_computation.5 | async-start | bytes 262144 | tf_op jit(solution)/shard_map/all_to_all | solution.py:72
  156.3 15.7 %all-to-all-start.6 = ((f32[8,32,256]{2,1,0:T(8,128)}), f32[8,32,256]{2,1,0:T(8,128)S(1)}, u32[]{:S(2)}, u32[]{:S(2)}) async-start(f32[8,32,256]{2,1,0:T(8,128)} %fusion.63), calls=%async_computation.6 | async-start | bytes 524288 | tf_op jit(solution)/shard_map/all_to_all | solution.py:54
  172.6 8.1 %all-to-all-start.7 = ((f32[4,2,16,256]{3,2,1,0:T(8,128)}), f32[4,2,16,256]{3,2,1,0:T(8,128)S(1)}, u32[]{:S(2)}, u32[]{:S(2)}) async-start(f32[4,2,16,256]{3,2,1,0:T(8,128)} %broadcast_in_dim.206), calls=%async_computation.7 | async-start | bytes 262144 | tf_op jit(solution)/shard_map/all_to_all | solution.py:72
  184.9 13.5 %copy-start.2 = (f32[2,128,16]{1,2,0:T(8,128)S(1)}, f32[2,128,16]{1,2,0:T(8,128)}, u32[]{:S(2)}) copy-start(f32[2,128,16]{1,2,0:T(8,128)} %param.12) | copy-start | bytes 49156
  185.6 12.8 %all-to-all-start.8 = ((f32[8,2,16,128]{3,2,1,0:T(8,128)}), f32[8,2,16,128]{3,2,1,0:T(8,128)S(1)}, u32[]{:S(2)}, u32[]{:S(2)}) async-start(f32[8,2,16,128]{3,2,1,0:T(8,128)} %copy.24), calls=%async_computation.8 | async-start | bytes 262144 | tf_op jit(solution)/shard_map/all_to_all | solution.py:54

commit v2 on v1

--- a/solution.py
+++ b/solution.py
@@ -54,12 +54,13 @@
     return jnp.sum(lax.all_to_all(parts, axis, 0, 0, tiled=True), axis=0)
 
 
-def turn(value, count):
-    places = [(i, j) for i in range(count) for j in range(count)]
-    for goes in (lambda i, j: ((i + j) % count, j), lambda i, j: (i, (i - j) % count)):
-        order = [(i * count + j, goes(i, j)[0] * count + goes(i, j)[1]) for i, j in places]
-        value = lax.ppermute(value, ("y",) + WIN, order)
-    return value
+def shift(value, goes, count):
+    order = []
+    for i in range(count):
+        for j in range(count):
+            to_y, to_window = goes(i, j)
+            order.append((i * count + j, to_y * count + to_window))
+    return lax.ppermute(value, ("y",) + WIN, order)
 
 
 def in_order(parts, first):
@@ -110,22 +111,23 @@
     kids = jnp.transpose(panel_kids, (0, 2, 1)) * keep_rows[:, None, :]
     panel = jnp.concatenate([top_rows, kids.reshape(2 * kid_col, kid_own)], axis=1)
 
-    turned = turn(panel, ny)
-    other = swap(panel, "h")
+    kid_rows = lax.all_gather(kids, WIN + SUB, axis=1, tiled=True)
+    turned = shift(panel, lambda i, j: ((i + j) % ny, j), ny)
+    other = swap(top_rows, "h")
     near = lax.all_gather(field, "q", axis=0).reshape(nq * anc_col, live)
     near, other, turned = lax.optimization_barrier((near, other, turned))
+    turned = shift(turned, lambda i, j: (i, (i - j) % ny), ny)
     far = swap(near, "c")
-    pair = jnp.stack([jnp.where(h_id == 0, panel, other), jnp.where(h_id == 0, other, panel)])
-    turned = spread(turned, "y").reshape(ny * top_col, live + kid_own)
-    wide = spread(pair, "x").reshape(ny * top_col, live + kid_own)
-
-    top_wide = wide[:, :live]
+    pair = jnp.stack([jnp.where(h_id == 0, top_rows, other), jnp.where(h_id == 0, other, top_rows)])
+    top_wide = spread(pair, "x").reshape(ny * top_col, live)
+    top_wide, turned = lax.optimization_barrier((top_wide, turned))
     zed = select_exact(dot_nt(top_wide, near), near_choice) + select_exact(
         dot_nt(top_wide, far), far_choice
     )
+    zed = sum_over(zed.reshape(ny, top_col, live), "y")
     zed, turned = lax.optimization_barrier((zed, turned))
-    zed = sum_over(zed.reshape(ny, top_col, live), "y")
-    zed = gather_sub(zed).reshape(-1, live)
+    turned = spread(turned, "y").reshape(ny * top_col, live + kid_own)
+    zed = lax.all_gather(lax.all_gather(zed, "q", axis=0), "c", axis=1).reshape(-1, live)
     cross_top = -lax.dot_general(
         own_choice, jnp.concatenate(pieces(zed), axis=0), (((1,), (1,)), ((), ())),
         preferred_element_type=jnp.float32,
@@ -136,25 +138,30 @@
         in_order(part.reshape(nx * nh, top_col, -1), win_id), WIN
     )
 
-    block = gather_sub(sigma_top).reshape(-1, kid_own)
-    part = dot_nt(wide[:, live:], block)
-    zed = sum_over(part.reshape(ny, 2 * kid_col, -1), "y")
-    zed = gather_sub(zed.reshape(2, kid_col, -1))
-    zed = jnp.transpose(zed, (1, 0, 2, 3)).reshape(2, -1, kid_own)
+    part = dot_nt(sigma_top, kid_rows.reshape(-1, kid_own)).reshape(top_col, 2, ny, -1)
+    zed = sum_over(jnp.transpose(part, (2, 1, 0, 3)), "y")
     col_flags = lax.dynamic_slice_in_dim(flags_kids, win_id * kid_blocks + sub_id, 1, 1)
-    cross_kids = lax.dynamic_slice_in_dim(zed, sub_id * top_col, top_col, 2)
-    cross_kids = -(cross_kids * col_flags.astype(jnp.float32)[:, :, None])
+    cross_kids = -(zed * col_flags.astype(jnp.float32)[:, :, None])
 
+    zed = gather_sub(zed)
     turned_kids = turned[:, live:].reshape(nx * nh, 2, kid_col, kid_own)
     part = jnp.stack(
-        [dot_nt(turned_kids[:, k].reshape(-1, kid_own), zed[k]) for k in range(2)]
+        [
+            lax.dot(
+                turned_kids[:, k].reshape(-1, kid_own),
+                zed[:, k].reshape(kid_own, -1),
+                precision=HIGH,
+                preferred_element_type=jnp.float32,
+            )
+            for k in range(2)
+        ]
     )
     part = jnp.transpose(part.reshape(2, nx * nh, kid_col, -1), (1, 0, 2, 3))
     sigma_kids = jnp.transpose(pivot_kids, (0, 2, 1)) + sum_over(in_order(part, win_id), WIN)
     return (
         cross_top.T,
         sigma_top.T,
-        cross_kids,
+        jnp.transpose(cross_kids, (0, 2, 1)),
         jnp.transpose(sigma_kids, (0, 2, 1)),
     )
 

time: 200 us -> 190 us (0.950)
  waiting for transfers between devices: 59 us -> 33.6 us
  blocking collectives: 49.4 us -> 72 us
  starting transfers between devices: 68.7 us -> 48.9 us
  between operations: 1.08 us -> 14.5 us
  local copies, waits for them, and re-layouts: 8.43 us -> 6.37 us
    all_to_all x5 -> x3, waiting for transfers between devices: 29.3 us -> 7.27 us  [spread(): return lax.all_to_all(copies, axis, 0, 0, tiled=True)]
    all_to_all x5 -> x3, starting transfers between devices: 36.6 us -> 18.1 us  [spread(): return lax.all_to_all(copies, axis, 0, 0, tiled=True)]
    all_gather x0 -> x2, blocking collectives: none -> 18.3 us  [the longest x1 12.3 us: per_device(): lax.all_gather(zed, 'q', axis=0)]
    all_to_all x1, blocking collectives: 14.8 us -> 29.9 us  [sum_over(): return jnp.sum(lax.all_to_all(parts, axis, 0, 0, tiled=True), axis=0)]
    all_gather x3 -> x1, blocking collectives: 16.5 us -> 7.59 us  [gather_sub(): both = lax.all_gather(lines, 'c', axis=1)]
    all_to_all x3, waiting for transfers between devices: 29.6 us -> 26.3 us  [sum_over(): return jnp.sum(lax.all_to_all(parts, axis, 0, 0, tiled=True), axis=0)]
    ppermute x2, starting transfers between devices: 20.6 us -> 18.1 us  [swap(): return lax.ppermute(value, axis, [(0, 1), (1, 0)])]
    dot_general x6 -> x4, matrix products: 4.25 us -> 4.22 us  [dot_nt(): lax.dot_general(a, b, (((1,), (1,)), ((), ())), precision=HIGH, preferred...]
  transfers between devices with their start and end apart: 12 -> 11, of which waited for: 8 -> 5; matrix products, arithmetic and copies ran while one was open for 5% -> 6% of each run, Pallas kernels for 0% -> 0%
where the time goes in v2:
time: 190 us; the launch traced here: 189 us
  blocking collectives  72 us (38%)
  starting transfers between devices  48.9 us (26%)
  waiting for transfers between devices  33.6 us (18%)
  between operations  14.5 us (8%)
  other arithmetic  7.07 us (4%)
  matrix products  6.96 us (4%)
  local copies, waits for them, and re-layouts  6.37 us (3%)
    all_to_all x1, blocking collectives, sum_over(): return jnp.sum(lax.all_to_all(parts, axis, 0, 0, tiled=True), axis=0)  29.9 us
    all_to_all x3, waiting for transfers between devices, sum_over(): return jnp.sum(lax.all_to_all(parts, axis, 0, 0, tiled=True), axis=0)  26.3 us
    all_to_all x3, starting transfers between devices, spread(): return lax.all_to_all(copies, axis, 0, 0, tiled=True)  18.1 us
    ppermute x2, starting transfers between devices, swap(): return lax.ppermute(value, axis, [(0, 1), (1, 0)])  18.1 us
    all_gather x1, blocking collectives, per_device(): near = lax.all_gather(field, 'q', axis=0).reshape(nq * anc_col, live)  16.2 us
    all_gather x1, blocking collectives, per_device(): lax.all_gather(zed, 'q', axis=0)  12.3 us
    all_to_all x3, starting transfers between devices, sum_over(): return jnp.sum(lax.all_to_all(parts, axis, 0, 0, tiled=True), axis=0)  11.4 us
    all_gather x1, blocking collectives, gather_sub(): both = lax.all_gather(lines, 'c', axis=1)  7.59 us
  transfers between devices with their start and end apart: 11, of which 5 were waited for; matrix products, arithmetic and copies ran while one was open for 6% of the time, Pallas kernels for 0%

profile of v2, /device:TPU:1, one launch (start us, length us, event | category | flops | bytes accessed | tf_op | source)
XLA Modules:
  0.0 189.4 jit_solution(3075150112727011365)
XLA Ops:
  7.2 0.8 fusion.58
  8.6 1.1 reduce-precision_convert_fusion.7
  10.4 11.5 %collective-permute-start = (f32[32,512]{1,0:T(8,128)S(1)}, f32[32,512]{1,0:T(8,128)S(1)}, u32[]{:S(2)}, u32[]{:S(2)}) collective-permute-start(f32[32,512]{1,0:T(8,128)S(1)} %slice.71), channel_id=1, source_target_pairs={{0,8},{8,0},{1,9},{9,1},{2,10},{10,2},{3,11},{11,3},{4,12},{12,4},... | collective-permute-start | bytes 196616 | tf_op jit(solution)/shard_map/ppermute | solution.py:50
  23.9 16.2 %all-gather = f32[384,512]{1,0:T(8,128)S(1)} all-gather(f32[96,512]{1,0:T(8,128)S(1)} %slice.72), channel_id=2, replica_groups=mesh['y'=8,'x'=4,'h'=2,'q'=4,'c'=2] {'q'}, dimensions={0}, use_global_device_ids=true | all-gather | bytes 983040 | tf_op jit(solution)/shard_map/all_gather | solution.py:117
  40.1 0.9 broadcast_in_dim.181
  41.0 11.2 %all-to-all-start = ((f32[4,2,32,512]{3,2,1,0:T(8,128)}), f32[4,2,32,512]{3,2,1,0:T(8,128)S(1)}, u32[]{:S(2)}, u32[]{:S(2)}) async-start(f32[4,2,32,512]{3,2,1,0:T(8,128)} %broadcast_in_dim.181), calls=%async_computation | async-start | bytes 1048576 | tf_op jit(solution)/shard_map/all_to_all | solution.py:73
  52.2 6.6 %collective-permute-start.3 = (f32[384,512]{1,0:T(8,128)S(1)}, f32[384,512]{1,0:T(8,128)S(1)}, u32[]{:S(2)}, u32[]{:S(2)}) collective-permute-start(f32[384,512]{1,0:T(8,128)S(1)} %all-gather), channel_id=1, source_target_pairs={{0,1},{1,0},{2,3},{3,2},{4,5},{5,4},{6,7},{7,6},{8,9},{9,8},{10,11... | collective-permute-start | bytes 2359304 | tf_op jit(solution)/shard_map/ppermute | solution.py:50
  63.1 29.9 %all_to_all.35 = f32[8,32,512]{2,1,0:T(8,128)S(1)} all-to-all(f32[8,32,512]{2,1,0:T(8,128)S(1)} %bitcast.83), channel_id=1, replica_groups=mesh['y'=8,'x'=4,'h'=2,'q'=4,'c'=2] {'y'}, dimensions={0} | all-to-all | bytes 1048576 | tf_op jit(solution)/shard_map/all_to_all | solution.py:54
  93.1 1.0 broadcast_in_dim.189
  94.1 3.5 %all-to-all-start.2 = ((f32[8,32,768]{2,1,0:T(8,128)}), f32[8,32,768]{2,1,0:T(8,128)S(1)}, u32[]{:S(2)}, u32[]{:S(2)}) async-start(f32[8,32,768]{2,1,0:T(8,128)} %broadcast_in_dim.189), calls=%async_computation.2 | async-start | bytes 1572864 | tf_op jit(solution)/shard_map/all_to_all | solution.py:73
  97.8 12.3 %all-gather.1 = f32[128,512]{1,0:T(8,128)S(1)} all-gather(f32[32,512]{1,0:T(8,128)S(1)} %reduce_sum.117), channel_id=3, replica_groups=mesh['y'=8,'x'=4,'h'=2,'q'=4,'c'=2] {'q'}, dimensions={0}, use_global_device_ids=true | all-gather | bytes 327680 | tf_op jit(solution)/shard_map/all_gather | solution.py:130
  110.1 6.1 %all-gather.2 = f32[4,64,512]{2,1,0:T(8,128)S(1)} all-gather(f32[4,32,512]{2,1,0:T(8,128)S(1)} %bitcast.86), channel_id=4, replica_groups=mesh['y'=8,'x'=4,'h'=2,'q'=4,'c'=2] {'c'}, dimensions={1}, use_global_device_ids=true | all-gather | bytes 786432 | tf_op jit(solution)/shard_map/all_gather | solution.py:130
  116.2 3.2 %all-to-all-done.2 = f32[8,32,768]{2,1,0:T(8,128)S(1)} async-done(((f32[8,32,768]{2,1,0:T(8,128)}), f32[8,32,768]{2,1,0:T(8,128)S(1)}, u32[]{:S(2)}, u32[]{:S(2)}) %all-to-all-start.2) | async-done | bytes 786464 | tf_op jit(solution)/shard_map/all_to_all | solution.py:73
  119.8 0.8 fusion.34
  120.6 3.4 %all-to-all-start.3 = ((f32[8,32,256]{2,1,0:T(8,128)}), f32[8,32,256]{2,1,0:T(8,128)S(1)}, u32[]{:S(2)}, u32[]{:S(2)}) async-start(f32[8,32,256]{2,1,0:T(8,128)} %fusion.34), calls=%async_computation.3 | async-start | bytes 524288 | tf_op jit(solution)/shard_map/all_to_all | solution.py:54
  124.6 9.5 %all-to-all-done.3 = f32[8,32,256]{2,1,0:T(8,128)S(1)} async-done(((f32[8,32,256]{2,1,0:T(8,128)}), f32[8,32,256]{2,1,0:T(8,128)S(1)}, u32[]{:S(2)}, u32[]{:S(2)}) %all-to-all-start.3) | async-done | bytes 262176 | tf_op jit(solution)/shard_map/all_to_all | solution.py:54
  134.2 2.6 %convolution_bitcast_fusion = f32[8,2,32,128]{3,2,0,1:T(8,128)S(1)} fusion(f32[2,8,128,256]{3,2,1,0:T(8,128)} %bitcast.84, f32[32,256]{1,0:T(8,128)S(1)} %reduce_sum.119, f32[256,32]{0,1:T(8,128)S(1)} %copy-done), kind=kOutput, calls=%fused_computation.2 | convolution fusion | flops 100671488 | bytes 2424832 | tf_op jit(solution)/shard_map/dot_general | solution.py:15
  137.5 4.6 %all-to-all-start.4 = ((f32[8,2,32,128]{3,2,1,0:T(8,128)}), f32[8,2,32,128]{3,2,1,0:T(8,128)S(1)}, u32[]{:S(2)}, u32[]{:S(2)}) async-start(f32[8,2,32,128]{3,2,1,0:T(8,128)} %copy.17), calls=%async_computation.4 | async-start | bytes 524288 | tf_op jit(solution)/shard_map/all_to_all | solution.py:54
  143.0 8.6 %all-to-all-done.4 = f32[8,2,32,128]{3,2,1,0:T(8,128)S(1)} async-done(((f32[8,2,32,128]{3,2,1,0:T(8,128)}), f32[8,2,32,128]{3,2,1,0:T(8,128)S(1)}, u32[]{:S(2)}, u32[]{:S(2)}) %all-to-all-start.4) | async-done | bytes 262176 | tf_op jit(solution)/shard_map/all_to_all | solution.py:54
  152.2 3.3 %all-to-all-start.5 = ((f32[4,2,32,128]{3,2,1,0:T(8,128)}), f32[4,2,32,128]{3,2,1,0:T(8,128)S(1)}, u32[]{:S(2)}, u32[]{:S(2)}) async-start(f32[4,2,32,128]{3,2,1,0:T(8,128)} %broadcast_in_dim.190), calls=%async_computation.5 | async-start | bytes 262144 | tf_op jit(solution)/shard_map/all_to_all | solution.py:73
  156.3 4.1 %all-to-all-done.5 = f32[4,2,32,128]{3,2,1,0:T(8,128)S(1)} async-done(((f32[4,2,32,128]{3,2,1,0:T(8,128)}), f32[4,2,32,128]{3,2,1,0:T(8,128)S(1)}, u32[]{:S(2)}, u32[]{:S(2)}) %all-to-all-start.5) | async-done | bytes 131104 | tf_op jit(solution)/shard_map/all_to_all | solution.py:73
  160.3 7.6 %all-gather.3 = f32[4,4,32,128]{3,2,1,0:T(8,128)S(1)} all-gather(f32[4,2,32,128]{3,2,1,0:T(8,128)S(1)} %all-to-all-done.5), channel_id=5, replica_groups=mesh['y'=8,'x'=4,'h'=2,'q'=4,'c'=2] {'c'}, dimensions={1}, use_global_device_ids=true | all-gather | bytes 393216 | tf_op jit(solution)/shard_map/all_gather | solution.py:78
  169.1 3.4 %all-to-all-start.6 = ((f32[8,2,16,128]{3,2,1,0:T(8,128)}), f32[8,2,16,128]{3,2,1,0:T(8,128)S(1)}, u32[]{:S(2)}, u32[]{:S(2)}) async-start(f32[8,2,16,128]{3,2,1,0:T(8,128)} %copy.20), calls=%async_computation.6 | async-start | bytes 262144 | tf_op jit(solution)/shard_map/all_to_all | solution.py:54
  173.7 8.1 %all-to-all-done.6 = f32[8,2,16,128]{3,2,1,0:T(8,128)S(1)} async-done(((f32[8,2,16,128]{3,2,1,0:T(8,128)}), f32[8,2,16,128]{3,2,1,0:T(8,128)S(1)}, u32[]{:S(2)}, u32[]{:S(2)}) %all-to-all-start.6) | async-done | bytes 131104 | tf_op jit(solution)/shard_map/all_to_all | solution.py:54
  (96 shorter events, 14.7 us)
Async XLA Ops:
  7.2 127.0 %all-gather.6.cloned.1.call-start = ((), (), s32[]{:S(2)}) async-start(), calls=%async_computation.7 | async-start | bytes 2129920 | tf_op jit(solution)/shard_map/all_gather | solution.py:114
  9.7 12.2 %copy-start.3 = (s32[2,64]{1,0:T(2,128)S(1)}, s32[2,64]{1,0:T(2,128)}, u32[]{:S(2)}) copy-start(s32[2,64]{1,0:T(2,128)} %param.13) | copy-start | bytes 1540
  9.8 12.4 %copy-start.1 = (f32[2,256,16]{1,2,0:T(8,128)S(1)}, f32[2,256,16]{1,2,0:T(8,128)}, u32[]{:S(2)}) copy-start(f32[2,256,16]{1,2,0:T(8,128)} %param.11) | copy-start | bytes 98308
  10.4 29.7 %collective-permute-start = (f32[32,512]{1,0:T(8,128)S(1)}, f32[32,512]{1,0:T(8,128)S(1)}, u32[]{:S(2)}, u32[]{:S(2)}) collective-permute-start(f32[32,512]{1,0:T(8,128)S(1)} %slice.71), channel_id=1, source_target_pairs={{0,8},{8,0},{1,9},{9,1},{2,10},{10,2},{3,11},{11,3},{4,12},{12,4},... | collective-permute-start | bytes 196616 | tf_op jit(solution)/shard_map/ppermute | solution.py:50
  22.2 17.9 %collective-permute-start.1 = (f32[32,768]{1,0:T(8,128)S(1)}, f32[32,768]{1,0:T(8,128)S(1)}, u32[]{:S(2)}, u32[]{:S(2)}) collective-permute-start(f32[32,768]{1,0:T(8,128)S(1)} %pad_maximum_fusion.2), channel_id=1, source_target_pairs={{0,0},{8,72},{16,144},{24,216},{32,288},{40,360},{48,432},{56,504}... | collective-permute-start | bytes 294920 | tf_op jit(solution)/shard_map/ppermute | solution.py:63
  41.0 19.1 %all-to-all-start = ((f32[4,2,32,512]{3,2,1,0:T(8,128)}), f32[4,2,32,512]{3,2,1,0:T(8,128)S(1)}, u32[]{:S(2)}, u32[]{:S(2)}) async-start(f32[4,2,32,512]{3,2,1,0:T(8,128)} %broadcast_in_dim.181), calls=%async_computation | async-start | bytes 1048576 | tf_op jit(solution)/shard_map/all_to_all | solution.py:73
  52.2 9.3 %collective-permute-start.3 = (f32[384,512]{1,0:T(8,128)S(1)}, f32[384,512]{1,0:T(8,128)S(1)}, u32[]{:S(2)}, u32[]{:S(2)}) collective-permute-start(f32[384,512]{1,0:T(8,128)S(1)} %all-gather), channel_id=1, source_target_pairs={{0,1},{1,0},{2,3},{3,2},{4,5},{5,4},{6,7},{7,6},{8,9},{9,8},{10,11... | collective-permute-start | bytes 2359304 | tf_op jit(solution)/shard_map/ppermute | solution.py:50
  59.4 0.7 collective-permute-start.2
  94.1 25.3 %all-to-all-start.2 = ((f32[8,32,768]{2,1,0:T(8,128)}), f32[8,32,768]{2,1,0:T(8,128)S(1)}, u32[]{:S(2)}, u32[]{:S(2)}) async-start(f32[8,32,768]{2,1,0:T(8,128)} %broadcast_in_dim.189), calls=%async_computation.2 | async-start | bytes 1572864 | tf_op jit(solution)/shard_map/all_to_all | solution.py:73
  119.4 14.8 %copy-start = (f32[256,32]{0,1:T(8,128)S(1)}, f32[256,32]{0,1:T(8,128)}, u32[]{:S(2)}) copy-start(f32[256,32]{0,1:T(8,128)} %param.9) | copy-start | bytes 98308
  120.6 13.5 %all-to-all-start.3 = ((f32[8,32,256]{2,1,0:T(8,128)}), f32[8,32,256]{2,1,0:T(8,128)S(1)}, u32[]{:S(2)}, u32[]{:S(2)}) async-start(f32[8,32,256]{2,1,0:T(8,128)} %fusion.34), calls=%async_computation.3 | async-start | bytes 524288 | tf_op jit(solution)/shard_map/all_to_all | solution.py:54
  137.5 14.1 %all-to-all-start.4 = ((f32[8,2,32,128]{3,2,1,0:T(8,128)}), f32[8,2,32,128]{3,2,1,0:T(8,128)S(1)}, u32[]{:S(2)}, u32[]{:S(2)}) async-start(f32[8,2,32,128]{3,2,1,0:T(8,128)} %copy.17), calls=%async_computation.4 | async-start | bytes 524288 | tf_op jit(solution)/shard_map/all_to_all | solution.py:54
  152.2 8.1 %all-to-all-start.5 = ((f32[4,2,32,128]{3,2,1,0:T(8,128)}), f32[4,2,32,128]{3,2,1,0:T(8,128)S(1)}, u32[]{:S(2)}, u32[]{:S(2)}) async-start(f32[4,2,32,128]{3,2,1,0:T(8,128)} %broadcast_in_dim.190), calls=%async_computation.5 | async-start | bytes 262144 | tf_op jit(solution)/shard_map/all_to_all | solution.py:73
  156.2 25.7 %copy-start.2 = (f32[2,128,16]{1,2,0:T(8,128)S(1)}, f32[2,128,16]{1,2,0:T(8,128)}, u32[]{:S(2)}) copy-start(f32[2,128,16]{1,2,0:T(8,128)} %param.12) | copy-start | bytes 49156
  169.1 12.8 %all-to-all-start.6 = ((f32[8,2,16,128]{3,2,1,0:T(8,128)}), f32[8,2,16,128]{3,2,1,0:T(8,128)S(1)}, u32[]{:S(2)}, u32[]{:S(2)}) async-start(f32[8,2,16,128]{3,2,1,0:T(8,128)} %copy.20), calls=%async_computation.6 | async-start | bytes 262144 | tf_op jit(solution)/shard_map/all_to_all | solution.py:54
Sparse Core Ops, SparseCore 0:
  23.6 85.0 all-gather.5

commit v3 on v2

--- a/solution.py
+++ b/solution.py
@@ -114,16 +114,15 @@
     kid_rows = lax.all_gather(kids, WIN + SUB, axis=1, tiled=True)
     turned = shift(panel, lambda i, j: ((i + j) % ny, j), ny)
     other = swap(top_rows, "h")
-    near = lax.all_gather(field, "q", axis=0).reshape(nq * anc_col, live)
-    near, other, turned = lax.optimization_barrier((near, other, turned))
-    turned = shift(turned, lambda i, j: (i, (i - j) % ny), ny)
-    far = swap(near, "c")
+    field, other = lax.optimization_barrier((field, other))
     pair = jnp.stack([jnp.where(h_id == 0, top_rows, other), jnp.where(h_id == 0, other, top_rows)])
     top_wide = spread(pair, "x").reshape(ny * top_col, live)
-    top_wide, turned = lax.optimization_barrier((top_wide, turned))
-    zed = select_exact(dot_nt(top_wide, near), near_choice) + select_exact(
-        dot_nt(top_wide, far), far_choice
-    )
+    turned = shift(turned, lambda i, j: (i, (i - j) % ny), ny)
+    near = lax.all_gather(field, "q", axis=0).reshape(nq * anc_col, live)
+    near, top_wide, turned = lax.optimization_barrier((near, top_wide, turned))
+    far = swap(near, "c")
+    zed = jnp.concatenate([dot_nt(top_wide, near), dot_nt(top_wide, far)], axis=1)
+    zed = select_exact(zed, jnp.concatenate([near_choice, far_choice], axis=0))
     zed = sum_over(zed.reshape(ny, top_col, live), "y")
     zed, turned = lax.optimization_barrier((zed, turned))
     turned = spread(turned, "y").reshape(ny * top_col, live + kid_own)
@@ -134,11 +133,20 @@
     ).reshape(anc_col, 3, -1).sum(axis=1)
 
     part = dot_nt(turned[:, :live], zed)
+    part, kid_rows = lax.optimization_barrier((part, kid_rows))
+    kid_high, kid_low, _ = pieces(kid_rows.reshape(-1, kid_own))
+    kid_terms = jnp.concatenate([kid_high, kid_low, kid_high], axis=1)
     sigma_top = pivot_top.T + sum_over(
         in_order(part.reshape(nx * nh, top_col, -1), win_id), WIN
     )
 
-    part = dot_nt(sigma_top, kid_rows.reshape(-1, kid_own)).reshape(top_col, 2, ny, -1)
+    top_high, top_low, _ = pieces(sigma_top)
+    part = lax.dot_general(
+        jnp.concatenate([top_high, top_high, top_low], axis=1),
+        kid_terms,
+        (((1,), (1,)), ((), ())),
+        preferred_element_type=jnp.float32,
+    ).reshape(top_col, 2, ny, -1)
     zed = sum_over(jnp.transpose(part, (2, 1, 0, 3)), "y")
     col_flags = lax.dynamic_slice_in_dim(flags_kids, win_id * kid_blocks + sub_id, 1, 1)
     cross_kids = -(zed * col_flags.astype(jnp.float32)[:, :, None])

time: 190 us -> 189 us (level)
  blocking collectives: 72 us -> 68.7 us
  other arithmetic: 7.07 us -> 9.74 us
    convert_element_type x2 -> x5, other arithmetic: 1.21 us -> 4.28 us  [pieces(): return [part.astype(jnp.bfloat16) for part in (high, mid, rest - mid)]]
    all_to_all x1, blocking collectives: 29.9 us -> 26.9 us  [sum_over(): return jnp.sum(lax.all_to_all(parts, axis, 0, 0, tiled=True), axis=0)]
    dot_general x4 -> x3, matrix products: 4.22 us -> 1.61 us  [dot_nt(): lax.dot_general(a, b, (((1,), (1,)), ((), ())), precision=HIGH, preferred...]
    dot_general x0 -> x1, matrix products: none -> 2.56 us  [per_device(): lax.dot_general(jnp.concatenate([top_high, top_high, top_low], axis=1), k...]
    all_to_all x3, waiting for transfers between devices: 26.3 us -> 23.9 us  [sum_over(): return jnp.sum(lax.all_to_all(parts, axis, 0, 0, tiled=True), axis=0)]
  transfers between devices with their start and end apart: 11 -> 11, of which waited for: 5 -> 6; matrix products, arithmetic and copies ran while one was open for 6% -> 7% of each run, Pallas kernels for 0% -> 0%
where the time goes in v3:
time: 189 us; the launch traced here: 188 us
  blocking collectives  68.7 us (36%)
  starting transfers between devices  49.2 us (26%)
  waiting for transfers between devices  32.4 us (17%)
  between operations  14.5 us (8%)
  other arithmetic  9.74 us (5%)
  local copies, waits for them, and re-layouts  7.12 us (4%)
  matrix products  6.35 us (3%)
    all_to_all x1, blocking collectives, sum_over(): return jnp.sum(lax.all_to_all(parts, axis, 0, 0, tiled=True), axis=0)  26.9 us
    all_to_all x3, waiting for transfers between devices, sum_over(): return jnp.sum(lax.all_to_all(parts, axis, 0, 0, tiled=True), axis=0)  23.9 us
    ppermute x2, starting transfers between devices, swap(): return lax.ppermute(value, axis, [(0, 1), (1, 0)])  18.2 us
    all_to_all x3, starting transfers between devices, spread(): return lax.all_to_all(copies, axis, 0, 0, tiled=True)  17.7 us
    all_gather x1, blocking collectives, per_device(): near = lax.all_gather(field, 'q', axis=0).reshape(nq * anc_col, live)  16.6 us
    all_gather x1, blocking collectives, per_device(): lax.all_gather(zed, 'q', axis=0)  12.4 us
    all_to_all x3, starting transfers between devices, sum_over(): return jnp.sum(lax.all_to_all(parts, axis, 0, 0, tiled=True), axis=0)  11.9 us
    all_to_all x3, waiting for transfers between devices, spread(): return lax.all_to_all(copies, axis, 0, 0, tiled=True)  7.61 us
  transfers between devices with their start and end apart: 11, of which 6 were waited for; matrix products, arithmetic and copies ran while one was open for 7% of the time, Pallas kernels for 0%

profile of v3, /device:TPU:1, one launch (start us, length us, event | category | flops | bytes accessed | tf_op | source)
XLA Modules:
  0.0 188.1 jit_solution(14344646134901601051)
XLA Ops:
  8.6 1.1 reduce-precision_convert_fusion.6
  10.4 11.5 %collective-permute-start = (f32[32,512]{1,0:T(8,128)S(1)}, f32[32,512]{1,0:T(8,128)S(1)}, u32[]{:S(2)}, u32[]{:S(2)}) collective-permute-start(f32[32,512]{1,0:T(8,128)S(1)} %slice.60), channel_id=1, source_target_pairs={{0,8},{8,0},{1,9},{9,1},{2,10},{10,2},{3,11},{11,3},{4,12},{12,4},... | collective-permute-start | bytes 196616 | tf_op jit(solution)/shard_map/ppermute | solution.py:50
  24.0 0.9 broadcast_in_dim.180
  24.8 10.8 %all-to-all-start = ((f32[4,2,32,512]{3,2,1,0:T(8,128)}), f32[4,2,32,512]{3,2,1,0:T(8,128)S(1)}, u32[]{:S(2)}, u32[]{:S(2)}) async-start(f32[4,2,32,512]{3,2,1,0:T(8,128)} %broadcast_in_dim.180), calls=%async_computation | async-start | bytes 1048576 | tf_op jit(solution)/shard_map/all_to_all | solution.py:73
  36.9 16.6 %all-gather = f32[384,512]{1,0:T(8,128)S(1)} all-gather(f32[96,512]{1,0:T(8,128)S(1)} %slice.59), channel_id=2, replica_groups=mesh['y'=8,'x'=4,'h'=2,'q'=4,'c'=2] {'q'}, dimensions={0}, use_global_device_ids=true | all-gather | bytes 983040 | tf_op jit(solution)/shard_map/all_gather | solution.py:121
  53.5 6.8 %collective-permute-start.3 = (f32[384,512]{1,0:T(8,128)S(1)}, f32[384,512]{1,0:T(8,128)S(1)}, u32[]{:S(2)}, u32[]{:S(2)}) collective-permute-start(f32[384,512]{1,0:T(8,128)S(1)} %all-gather), channel_id=1, source_target_pairs={{0,1},{1,0},{2,3},{3,2},{4,5},{5,4},{6,7},{7,6},{8,9},{9,8},{10,11... | collective-permute-start | bytes 2359304 | tf_op jit(solution)/shard_map/ppermute | solution.py:50
  61.2 0.9 collective-permute-done.3
  63.9 26.9 %all_to_all.35 = f32[8,32,512]{2,1,0:T(8,128)S(1)} all-to-all(f32[8,32,512]{2,1,0:T(8,128)S(1)} %bitcast.79), channel_id=1, replica_groups=mesh['y'=8,'x'=4,'h'=2,'q'=4,'c'=2] {'y'}, dimensions={0} | all-to-all | bytes 1048576 | tf_op jit(solution)/shard_map/all_to_all | solution.py:54
  90.9 1.0 broadcast_in_dim.189
  91.8 3.5 %all-to-all-start.2 = ((f32[8,32,768]{2,1,0:T(8,128)}), f32[8,32,768]{2,1,0:T(8,128)S(1)}, u32[]{:S(2)}, u32[]{:S(2)}) async-start(f32[8,32,768]{2,1,0:T(8,128)} %broadcast_in_dim.189), calls=%async_computation.2 | async-start | bytes 1572864 | tf_op jit(solution)/shard_map/all_to_all | solution.py:73
  96.1 12.4 %all-gather.1 = f32[128,512]{1,0:T(8,128)S(1)} all-gather(f32[32,512]{1,0:T(8,128)S(1)} %reduce_sum.117), channel_id=3, replica_groups=mesh['y'=8,'x'=4,'h'=2,'q'=4,'c'=2] {'q'}, dimensions={0}, use_global_device_ids=true | all-gather | bytes 327680 | tf_op jit(solution)/shard_map/all_gather | solution.py:129
  108.6 5.7 %all-gather.2 = f32[4,64,512]{2,1,0:T(8,128)S(1)} all-gather(f32[4,32,512]{2,1,0:T(8,128)S(1)} %bitcast.81), channel_id=4, replica_groups=mesh['y'=8,'x'=4,'h'=2,'q'=4,'c'=2] {'c'}, dimensions={1}, use_global_device_ids=true | all-gather | bytes 786432 | tf_op jit(solution)/shard_map/all_gather | solution.py:129
  114.2 3.5 %all-to-all-done.2 = f32[8,32,768]{2,1,0:T(8,128)S(1)} async-done(((f32[8,32,768]{2,1,0:T(8,128)}), f32[8,32,768]{2,1,0:T(8,128)S(1)}, u32[]{:S(2)}, u32[]{:S(2)}) %all-to-all-start.2) | async-done | bytes 786464 | tf_op jit(solution)/shard_map/all_to_all | solution.py:73
  119.0 4.8 %all-to-all-start.3 = ((f32[8,32,256]{2,1,0:T(8,128)}), f32[8,32,256]{2,1,0:T(8,128)S(1)}, u32[]{:S(2)}, u32[]{:S(2)}) async-start(f32[8,32,256]{2,1,0:T(8,128)} %fusion.39), calls=%async_computation.3 | async-start | bytes 524288 | tf_op jit(solution)/shard_map/all_to_all | solution.py:54
  123.8 2.9 %fusion.7 = (bf16[2048,256]{1,0:T(8,128)(2,1)S(1)}, bf16[2048,256]{1,0:T(8,128)(2,1)}) fusion(f32[2,1024,256]{2,1,0:T(8,128)} %all-gather.6.cloned.1.call-done), kind=kLoop, calls=%fused_computation.9 | loop fusion | flops 2621440 | bytes 4194304 | tf_op jit(solution)/shard_map/convert_element_type | solution.py:24
  126.7 7.2 %all-to-all-done.3 = f32[8,32,256]{2,1,0:T(8,128)S(1)} async-done(((f32[8,32,256]{2,1,0:T(8,128)}), f32[8,32,256]{2,1,0:T(8,128)S(1)}, u32[]{:S(2)}, u32[]{:S(2)}) %all-to-all-start.3) | async-done | bytes 262176 | tf_op jit(solution)/shard_map/all_to_all | solution.py:54
  134.0 2.6 %fusion.18 = f32[4,8,16,128]{3,1,2,0:T(8,128)S(1)} fusion(bf16[2048,256]{1,0:T(8,128)(2,1)} %get-tuple-element.33, bf16[2048,256]{1,0:T(8,128)(2,1)S(1)} %get-tuple-element.32, bf16[32,256]{1,0:T(8,128)(2,1)S(1)} %get-tuple-element.48, bf16[32,256]{1,0:T(8,128)(2,1)S(1)} %get-tuple-element.47), kind=kOutput, calls=%fused_computation.21 | convolution fusion | flops 110247936 | bytes 2392064 | tf_op jit(solution)/shard_map/dot_general | solution.py:144
  137.5 3.7 %all-to-all-start.4 = ((f32[8,2,32,128]{3,1,2,0:T(2,128)}), f32[8,2,32,128]{3,1,2,0:T(2,128)S(1)}, u32[]{:S(2)}, u32[]{:S(2)}) async-start(f32[8,2,32,128]{3,1,2,0:T(2,128)} %bitcast.73), calls=%async_computation.4 | async-start | bytes 524288 | tf_op jit(solution)/shard_map/all_to_all | solution.py:54
  142.1 8.5 %all-to-all-done.4 = f32[8,2,32,128]{3,1,2,0:T(2,128)S(1)} async-done(((f32[8,2,32,128]{3,1,2,0:T(2,128)}), f32[8,2,32,128]{3,1,2,0:T(2,128)S(1)}, u32[]{:S(2)}, u32[]{:S(2)}) %all-to-all-start.4) | async-done | bytes 262176 | tf_op jit(solution)/shard_map/all_to_all | solution.py:54
  151.4 3.3 %all-to-all-start.5 = ((f32[4,2,32,128]{3,2,1,0:T(8,128)}), f32[4,2,32,128]{3,2,1,0:T(8,128)S(1)}, u32[]{:S(2)}, u32[]{:S(2)}) async-start(f32[4,2,32,128]{3,2,1,0:T(8,128)} %broadcast_in_dim.190), calls=%async_computation.5 | async-start | bytes 262144 | tf_op jit(solution)/shard_map/all_to_all | solution.py:73
  155.4 4.1 %all-to-all-done.5 = f32[4,2,32,128]{3,2,1,0:T(8,128)S(1)} async-done(((f32[4,2,32,128]{3,2,1,0:T(8,128)}), f32[4,2,32,128]{3,2,1,0:T(8,128)S(1)}, u32[]{:S(2)}, u32[]{:S(2)}) %all-to-all-start.5) | async-done | bytes 131104 | tf_op jit(solution)/shard_map/all_to_all | solution.py:73
  159.5 7.2 %all-gather.3 = f32[4,4,32,128]{3,2,1,0:T(8,128)S(1)} all-gather(f32[4,2,32,128]{3,2,1,0:T(8,128)S(1)} %all-to-all-done.5), channel_id=5, replica_groups=mesh['y'=8,'x'=4,'h'=2,'q'=4,'c'=2] {'c'}, dimensions={1}, use_global_device_ids=true | all-gather | bytes 393216 | tf_op jit(solution)/shard_map/all_gather | solution.py:78
  167.8 3.4 %all-to-all-start.6 = ((f32[8,2,16,128]{3,2,1,0:T(8,128)}), f32[8,2,16,128]{3,2,1,0:T(8,128)S(1)}, u32[]{:S(2)}, u32[]{:S(2)}) async-start(f32[8,2,16,128]{3,2,1,0:T(8,128)} %copy.25), calls=%async_computation.6 | async-start | bytes 262144 | tf_op jit(solution)/shard_map/all_to_all | solution.py:54
  172.5 8.1 %all-to-all-done.6 = f32[8,2,16,128]{3,2,1,0:T(8,128)S(1)} async-done(((f32[8,2,16,128]{3,2,1,0:T(8,128)}), f32[8,2,16,128]{3,2,1,0:T(8,128)S(1)}, u32[]{:S(2)}, u32[]{:S(2)}) %all-to-all-start.6) | async-done | bytes 131104 | tf_op jit(solution)/shard_map/all_to_all | solution.py:54
  (102 shorter events, 16.2 us)
Async XLA Ops:
  7.2 111.1 %all-gather.6.cloned.1.call-start = ((), (), s32[]{:S(2)}) async-start(), calls=%async_computation.7 | async-start | bytes 2129920 | tf_op jit(solution)/shard_map/all_gather | solution.py:114
  9.7 12.2 %copy-start.3 = (s32[2,64]{1,0:T(2,128)S(1)}, s32[2,64]{1,0:T(2,128)}, u32[]{:S(2)}) copy-start(s32[2,64]{1,0:T(2,128)} %param.13) | copy-start | bytes 1540
  9.7 12.4 %copy-start.1 = (f32[2,256,16]{1,2,0:T(8,128)S(1)}, f32[2,256,16]{1,2,0:T(8,128)}, u32[]{:S(2)}) copy-start(f32[2,256,16]{1,2,0:T(8,128)} %param.11) | copy-start | bytes 98308
  10.4 13.5 %collective-permute-start = (f32[32,512]{1,0:T(8,128)S(1)}, f32[32,512]{1,0:T(8,128)S(1)}, u32[]{:S(2)}, u32[]{:S(2)}) collective-permute-start(f32[32,512]{1,0:T(8,128)S(1)} %slice.60), channel_id=1, source_target_pairs={{0,8},{8,0},{1,9},{9,1},{2,10},{10,2},{3,11},{11,3},{4,12},{12,4},... | collective-permute-start | bytes 196616 | tf_op jit(solution)/shard_map/ppermute | solution.py:50
  22.2 14.1 %collective-permute-start.1 = (f32[32,768]{1,0:T(8,128)S(1)}, f32[32,768]{1,0:T(8,128)S(1)}, u32[]{:S(2)}, u32[]{:S(2)}) collective-permute-start(f32[32,768]{1,0:T(8,128)S(1)} %pad_maximum_fusion.3), channel_id=1, source_target_pairs={{0,0},{8,72},{16,144},{24,216},{32,288},{40,360},{48,432},{56,504}... | collective-permute-start | bytes 294920 | tf_op jit(solution)/shard_map/ppermute | solution.py:63
  24.8 28.7 %all-to-all-start = ((f32[4,2,32,512]{3,2,1,0:T(8,128)}), f32[4,2,32,512]{3,2,1,0:T(8,128)S(1)}, u32[]{:S(2)}, u32[]{:S(2)}) async-start(f32[4,2,32,512]{3,2,1,0:T(8,128)} %broadcast_in_dim.180), calls=%async_computation | async-start | bytes 1048576 | tf_op jit(solution)/shard_map/all_to_all | solution.py:73
  36.3 17.2 %collective-permute-start.2 = (f32[32,768]{1,0:T(8,128)S(1)}, f32[32,768]{1,0:T(8,128)S(1)}, u32[]{:S(2)}, u32[]{:S(2)}) collective-permute-start(f32[32,768]{1,0:T(8,128)S(1)} %collective-permute-done.1), channel_id=1, source_target_pairs={{0,0},{8,56},{16,48},{24,40},{32,32},{40,24},{48,16},{56,8},{64,72... | collective-permute-start | bytes 294920 | tf_op jit(solution)/shard_map/ppermute | solution.py:63
  53.5 8.7 %collective-permute-start.3 = (f32[384,512]{1,0:T(8,128)S(1)}, f32[384,512]{1,0:T(8,128)S(1)}, u32[]{:S(2)}, u32[]{:S(2)}) collective-permute-start(f32[384,512]{1,0:T(8,128)S(1)} %all-gather), channel_id=1, source_target_pairs={{0,1},{1,0},{2,3},{3,2},{4,5},{5,4},{6,7},{7,6},{8,9},{9,8},{10,11... | collective-permute-start | bytes 2359304 | tf_op jit(solution)/shard_map/ppermute | solution.py:50
  91.8 25.9 %all-to-all-start.2 = ((f32[8,32,768]{2,1,0:T(8,128)}), f32[8,32,768]{2,1,0:T(8,128)S(1)}, u32[]{:S(2)}, u32[]{:S(2)}) async-start(f32[8,32,768]{2,1,0:T(8,128)} %broadcast_in_dim.189), calls=%async_computation.2 | async-start | bytes 1572864 | tf_op jit(solution)/shard_map/all_to_all | solution.py:73
  119.0 15.0 %all-to-all-start.3 = ((f32[8,32,256]{2,1,0:T(8,128)}), f32[8,32,256]{2,1,0:T(8,128)S(1)}, u32[]{:S(2)}, u32[]{:S(2)}) async-start(f32[8,32,256]{2,1,0:T(8,128)} %fusion.39), calls=%async_computation.3 | async-start | bytes 524288 | tf_op jit(solution)/shard_map/all_to_all | solution.py:54
  123.8 10.1 %copy-start = (f32[256,32]{0,1:T(8,128)S(1)}, f32[256,32]{0,1:T(8,128)}, u32[]{:S(2)}) copy-start(f32[256,32]{0,1:T(8,128)} %param.9) | copy-start | bytes 98308
  137.5 13.2 %all-to-all-start.4 = ((f32[8,2,32,128]{3,1,2,0:T(2,128)}), f32[8,2,32,128]{3,1,2,0:T(2,128)S(1)}, u32[]{:S(2)}, u32[]{:S(2)}) async-start(f32[8,2,32,128]{3,1,2,0:T(2,128)} %bitcast.73), calls=%async_computation.4 | async-start | bytes 524288 | tf_op jit(solution)/shard_map/all_to_all | solution.py:54
  150.7 29.9 %copy-start.2 = (f32[2,128,16]{1,2,0:T(8,128)S(1)}, f32[2,128,16]{1,2,0:T(8,128)}, u32[]{:S(2)}) copy-start(f32[2,128,16]{1,2,0:T(8,128)} %param.12) | copy-start | bytes 49156
  151.4 8.1 %all-to-all-start.5 = ((f32[4,2,32,128]{3,2,1,0:T(8,128)}), f32[4,2,32,128]{3,2,1,0:T(8,128)S(1)}, u32[]{:S(2)}, u32[]{:S(2)}) async-start(f32[4,2,32,128]{3,2,1,0:T(8,128)} %broadcast_in_dim.190), calls=%async_computation.5 | async-start | bytes 262144 | tf_op jit(solution)/shard_map/all_to_all | solution.py:73
  167.8 12.8 %all-to-all-start.6 = ((f32[8,2,16,128]{3,2,1,0:T(8,128)}), f32[8,2,16,128]{3,2,1,0:T(8,128)S(1)}, u32[]{:S(2)}, u32[]{:S(2)}) async-start(f32[8,2,16,128]{3,2,1,0:T(8,128)} %copy.25), calls=%async_computation.6 | async-start | bytes 262144 | tf_op jit(solution)/shard_map/all_to_all | solution.py:54
Sparse Core Ops, SparseCore 0:
  23.6 85.1 all-gather.5

commit v4 on v3

--- a/solution.py
+++ b/solution.py
@@ -121,11 +121,12 @@
     near = lax.all_gather(field, "q", axis=0).reshape(nq * anc_col, live)
     near, top_wide, turned = lax.optimization_barrier((near, top_wide, turned))
     far = swap(near, "c")
+    copies = jnp.broadcast_to(turned[None], (ny,) + turned.shape)
     zed = jnp.concatenate([dot_nt(top_wide, near), dot_nt(top_wide, far)], axis=1)
     zed = select_exact(zed, jnp.concatenate([near_choice, far_choice], axis=0))
     zed = sum_over(zed.reshape(ny, top_col, live), "y")
-    zed, turned = lax.optimization_barrier((zed, turned))
-    turned = spread(turned, "y").reshape(ny * top_col, live + kid_own)
+    zed, copies = lax.optimization_barrier((zed, copies))
+    turned = lax.all_to_all(copies, "y", 0, 0, tiled=True).reshape(ny * top_col, live + kid_own)
     zed = lax.all_gather(lax.all_gather(zed, "q", axis=0), "c", axis=1).reshape(-1, live)
     cross_top = -lax.dot_general(
         own_choice, jnp.concatenate(pieces(zed), axis=0), (((1,), (1,)), ((), ())),

time: 189 us -> 189 us (level)
    all_to_all x0 -> x1, starting transfers between devices: none -> 3.55 us  [per_device(): lax.all_to_all(copies, 'y', 0, 0, tiled=True)]
    all_to_all x3 -> x2, starting transfers between devices: 17.7 us -> 14.1 us  [spread(): return lax.all_to_all(copies, axis, 0, 0, tiled=True)]
    all_to_all x0 -> x1, waiting for transfers between devices: none -> 3.54 us  [per_device(): lax.all_to_all(copies, 'y', 0, 0, tiled=True)]
    all_to_all x3 -> x2, waiting for transfers between devices: 7.61 us -> 4.07 us  [spread(): return lax.all_to_all(copies, axis, 0, 0, tiled=True)]
where the time goes in v4:
time: 189 us; the launch traced here: 188 us
  blocking collectives  68.7 us (36%)
  starting transfers between devices  49.2 us (26%)
  waiting for transfers between devices  32.4 us (17%)
  between operations  14.5 us (8%)
  other arithmetic  9.74 us (5%)
  local copies, waits for them, and re-layouts  7.12 us (4%)
  matrix products  6.35 us (3%)
    all_to_all x1, blocking collectives, sum_over(): return jnp.sum(lax.all_to_all(parts, axis, 0, 0, tiled=True), axis=0)  26.9 us
    all_to_all x3, waiting for transfers between devices, sum_over(): return jnp.sum(lax.all_to_all(parts, axis, 0, 0, tiled=True), axis=0)  23.9 us
    ppermute x2, starting transfers between devices, swap(): return lax.ppermute(value, axis, [(0, 1), (1, 0)])  18.2 us
    all_gather x1, blocking collectives, per_device(): near = lax.all_gather(field, 'q', axis=0).reshape(nq * anc_col, live)  16.6 us
    all_to_all x2, starting transfers between devices, spread(): return lax.all_to_all(copies, axis, 0, 0, tiled=True)  14.1 us
    all_gather x1, blocking collectives, per_device(): lax.all_gather(zed, 'q', axis=0)  12.4 us
    all_to_all x3, starting transfers between devices, sum_over(): return jnp.sum(lax.all_to_all(parts, axis, 0, 0, tiled=True), axis=0)  11.9 us
    all_gather x1, blocking collectives, gather_sub(): both = lax.all_gather(lines, 'c', axis=1)  7.16 us
  transfers between devices with their start and end apart: 11, of which 6 were waited for; matrix products, arithmetic and copies ran while one was open for 7% of the time, Pallas kernels for 0%

profile of v4, /device:TPU:1, one launch (start us, length us, event | category | flops | bytes accessed | tf_op | source)
XLA Modules:
  0.0 188.1 jit_solution(14344646134901601051)
XLA Ops:
  8.6 1.1 reduce-precision_convert_fusion.6
  10.4 11.5 %collective-permute-start = (f32[32,512]{1,0:T(8,128)S(1)}, f32[32,512]{1,0:T(8,128)S(1)}, u32[]{:S(2)}, u32[]{:S(2)}) collective-permute-start(f32[32,512]{1,0:T(8,128)S(1)} %slice.60), channel_id=1, source_target_pairs={{0,8},{8,0},{1,9},{9,1},{2,10},{10,2},{3,11},{11,3},{4,12},{12,4},... | collective-permute-start | bytes 196616 | tf_op jit(solution)/shard_map/ppermute | solution.py:50
  24.0 0.9 broadcast_in_dim.180
  24.8 10.8 %all-to-all-start = ((f32[4,2,32,512]{3,2,1,0:T(8,128)}), f32[4,2,32,512]{3,2,1,0:T(8,128)S(1)}, u32[]{:S(2)}, u32[]{:S(2)}) async-start(f32[4,2,32,512]{3,2,1,0:T(8,128)} %broadcast_in_dim.180), calls=%async_computation | async-start | bytes 1048576 | tf_op jit(solution)/shard_map/all_to_all | solution.py:73
  36.9 16.6 %all-gather = f32[384,512]{1,0:T(8,128)S(1)} all-gather(f32[96,512]{1,0:T(8,128)S(1)} %slice.59), channel_id=2, replica_groups=mesh['y'=8,'x'=4,'h'=2,'q'=4,'c'=2] {'q'}, dimensions={0}, use_global_device_ids=true | all-gather | bytes 983040 | tf_op jit(solution)/shard_map/all_gather | solution.py:121
  53.5 6.8 %collective-permute-start.3 = (f32[384,512]{1,0:T(8,128)S(1)}, f32[384,512]{1,0:T(8,128)S(1)}, u32[]{:S(2)}, u32[]{:S(2)}) collective-permute-start(f32[384,512]{1,0:T(8,128)S(1)} %all-gather), channel_id=1, source_target_pairs={{0,1},{1,0},{2,3},{3,2},{4,5},{5,4},{6,7},{7,6},{8,9},{9,8},{10,11... | collective-permute-start | bytes 2359304 | tf_op jit(solution)/shard_map/ppermute | solution.py:50
  61.2 0.9 collective-permute-done.3
  63.9 26.9 %all_to_all.35 = f32[8,32,512]{2,1,0:T(8,128)S(1)} all-to-all(f32[8,32,512]{2,1,0:T(8,128)S(1)} %bitcast.79), channel_id=1, replica_groups=mesh['y'=8,'x'=4,'h'=2,'q'=4,'c'=2] {'y'}, dimensions={0} | all-to-all | bytes 1048576 | tf_op jit(solution)/shard_map/all_to_all | solution.py:54
  90.9 1.0 broadcast_in_dim.189
  91.8 3.5 %all-to-all-start.2 = ((f32[8,32,768]{2,1,0:T(8,128)}), f32[8,32,768]{2,1,0:T(8,128)S(1)}, u32[]{:S(2)}, u32[]{:S(2)}) async-start(f32[8,32,768]{2,1,0:T(8,128)} %broadcast_in_dim.189), calls=%async_computation.2 | async-start | bytes 1572864 | tf_op jit(solution)/shard_map/all_to_all | solution.py:129
  96.1 12.4 %all-gather.1 = f32[128,512]{1,0:T(8,128)S(1)} all-gather(f32[32,512]{1,0:T(8,128)S(1)} %reduce_sum.117), channel_id=3, replica_groups=mesh['y'=8,'x'=4,'h'=2,'q'=4,'c'=2] {'q'}, dimensions={0}, use_global_device_ids=true | all-gather | bytes 327680 | tf_op jit(solution)/shard_map/all_gather | solution.py:130
  108.6 5.7 %all-gather.2 = f32[4,64,512]{2,1,0:T(8,128)S(1)} all-gather(f32[4,32,512]{2,1,0:T(8,128)S(1)} %bitcast.81), channel_id=4, replica_groups=mesh['y'=8,'x'=4,'h'=2,'q'=4,'c'=2] {'c'}, dimensions={1}, use_global_device_ids=true | all-gather | bytes 786432 | tf_op jit(solution)/shard_map/all_gather | solution.py:130
  114.2 3.5 %all-to-all-done.2 = f32[8,32,768]{2,1,0:T(8,128)S(1)} async-done(((f32[8,32,768]{2,1,0:T(8,128)}), f32[8,32,768]{2,1,0:T(8,128)S(1)}, u32[]{:S(2)}, u32[]{:S(2)}) %all-to-all-start.2) | async-done | bytes 786464 | tf_op jit(solution)/shard_map/all_to_all | solution.py:129
  119.0 4.8 %all-to-all-start.3 = ((f32[8,32,256]{2,1,0:T(8,128)}), f32[8,32,256]{2,1,0:T(8,128)S(1)}, u32[]{:S(2)}, u32[]{:S(2)}) async-start(f32[8,32,256]{2,1,0:T(8,128)} %fusion.39), calls=%async_computation.3 | async-start | bytes 524288 | tf_op jit(solution)/shard_map/all_to_all | solution.py:54
  123.8 2.9 %fusion.7 = (bf16[2048,256]{1,0:T(8,128)(2,1)S(1)}, bf16[2048,256]{1,0:T(8,128)(2,1)}) fusion(f32[2,1024,256]{2,1,0:T(8,128)} %all-gather.6.cloned.1.call-done), kind=kLoop, calls=%fused_computation.9 | loop fusion | flops 2621440 | bytes 4194304 | tf_op jit(solution)/shard_map/convert_element_type | solution.py:24
  126.7 7.2 %all-to-all-done.3 = f32[8,32,256]{2,1,0:T(8,128)S(1)} async-done(((f32[8,32,256]{2,1,0:T(8,128)}), f32[8,32,256]{2,1,0:T(8,128)S(1)}, u32[]{:S(2)}, u32[]{:S(2)}) %all-to-all-start.3) | async-done | bytes 262176 | tf_op jit(solution)/shard_map/all_to_all | solution.py:54
  134.0 2.6 %fusion.18 = f32[4,8,16,128]{3,1,2,0:T(8,128)S(1)} fusion(bf16[2048,256]{1,0:T(8,128)(2,1)} %get-tuple-element.33, bf16[2048,256]{1,0:T(8,128)(2,1)S(1)} %get-tuple-element.32, bf16[32,256]{1,0:T(8,128)(2,1)S(1)} %get-tuple-element.48, bf16[32,256]{1,0:T(8,128)(2,1)S(1)} %get-tuple-element.47), kind=kOutput, calls=%fused_computation.21 | convolution fusion | flops 110247936 | bytes 2392064 | tf_op jit(solution)/shard_map/dot_general | solution.py:145
  137.5 3.7 %all-to-all-start.4 = ((f32[8,2,32,128]{3,1,2,0:T(2,128)}), f32[8,2,32,128]{3,1,2,0:T(2,128)S(1)}, u32[]{:S(2)}, u32[]{:S(2)}) async-start(f32[8,2,32,128]{3,1,2,0:T(2,128)} %bitcast.73), calls=%async_computation.4 | async-start | bytes 524288 | tf_op jit(solution)/shard_map/all_to_all | solution.py:54
  142.1 8.5 %all-to-all-done.4 = f32[8,2,32,128]{3,1,2,0:T(2,128)S(1)} async-done(((f32[8,2,32,128]{3,1,2,0:T(2,128)}), f32[8,2,32,128]{3,1,2,0:T(2,128)S(1)}, u32[]{:S(2)}, u32[]{:S(2)}) %all-to-all-start.4) | async-done | bytes 262176 | tf_op jit(solution)/shard_map/all_to_all | solution.py:54
  151.4 3.3 %all-to-all-start.5 = ((f32[4,2,32,128]{3,2,1,0:T(8,128)}), f32[4,2,32,128]{3,2,1,0:T(8,128)S(1)}, u32[]{:S(2)}, u32[]{:S(2)}) async-start(f32[4,2,32,128]{3,2,1,0:T(8,128)} %broadcast_in_dim.190), calls=%async_computation.5 | async-start | bytes 262144 | tf_op jit(solution)/shard_map/all_to_all | solution.py:73
  155.4 4.1 %all-to-all-done.5 = f32[4,2,32,128]{3,2,1,0:T(8,128)S(1)} async-done(((f32[4,2,32,128]{3,2,1,0:T(8,128)}), f32[4,2,32,128]{3,2,1,0:T(8,128)S(1)}, u32[]{:S(2)}, u32[]{:S(2)}) %all-to-all-start.5) | async-done | bytes 131104 | tf_op jit(solution)/shard_map/all_to_all | solution.py:73
  159.5 7.2 %all-gather.3 = f32[4,4,32,128]{3,2,1,0:T(8,128)S(1)} all-gather(f32[4,2,32,128]{3,2,1,0:T(8,128)S(1)} %all-to-all-done.5), channel_id=5, replica_groups=mesh['y'=8,'x'=4,'h'=2,'q'=4,'c'=2] {'c'}, dimensions={1}, use_global_device_ids=true | all-gather | bytes 393216 | tf_op jit(solution)/shard_map/all_gather | solution.py:78
  167.8 3.4 %all-to-all-start.6 = ((f32[8,2,16,128]{3,2,1,0:T(8,128)}), f32[8,2,16,128]{3,2,1,0:T(8,128)S(1)}, u32[]{:S(2)}, u32[]{:S(2)}) async-start(f32[8,2,16,128]{3,2,1,0:T(8,128)} %copy.25), calls=%async_computation.6 | async-start | bytes 262144 | tf_op jit(solution)/shard_map/all_to_all | solution.py:54
  172.5 8.1 %all-to-all-done.6 = f32[8,2,16,128]{3,2,1,0:T(8,128)S(1)} async-done(((f32[8,2,16,128]{3,2,1,0:T(8,128)}), f32[8,2,16,128]{3,2,1,0:T(8,128)S(1)}, u32[]{:S(2)}, u32[]{:S(2)}) %all-to-all-start.6) | async-done | bytes 131104 | tf_op jit(solution)/shard_map/all_to_all | solution.py:54
  (102 shorter events, 16.2 us)
Async XLA Ops:
  7.2 111.1 %all-gather.6.cloned.1.call-start = ((), (), s32[]{:S(2)}) async-start(), calls=%async_computation.7 | async-start | bytes 2129920 | tf_op jit(solution)/shard_map/all_gather | solution.py:114
  9.7 12.2 %copy-start.3 = (s32[2,64]{1,0:T(2,128)S(1)}, s32[2,64]{1,0:T(2,128)}, u32[]{:S(2)}) copy-start(s32[2,64]{1,0:T(2,128)} %param.13) | copy-start | bytes 1540
  9.7 12.4 %copy-start.1 = (f32[2,256,16]{1,2,0:T(8,128)S(1)}, f32[2,256,16]{1,2,0:T(8,128)}, u32[]{:S(2)}) copy-start(f32[2,256,16]{1,2,0:T(8,128)} %param.11) | copy-start | bytes 98308
  10.4 13.5 %collective-permute-start = (f32[32,512]{1,0:T(8,128)S(1)}, f32[32,512]{1,0:T(8,128)S(1)}, u32[]{:S(2)}, u32[]{:S(2)}) collective-permute-start(f32[32,512]{1,0:T(8,128)S(1)} %slice.60), channel_id=1, source_target_pairs={{0,8},{8,0},{1,9},{9,1},{2,10},{10,2},{3,11},{11,3},{4,12},{12,4},... | collective-permute-start | bytes 196616 | tf_op jit(solution)/shard_map/ppermute | solution.py:50
  22.2 14.1 %collective-permute-start.1 = (f32[32,768]{1,0:T(8,128)S(1)}, f32[32,768]{1,0:T(8,128)S(1)}, u32[]{:S(2)}, u32[]{:S(2)}) collective-permute-start(f32[32,768]{1,0:T(8,128)S(1)} %pad_maximum_fusion.3), channel_id=1, source_target_pairs={{0,0},{8,72},{16,144},{24,216},{32,288},{40,360},{48,432},{56,504}... | collective-permute-start | bytes 294920 | tf_op jit(solution)/shard_map/ppermute | solution.py:63
  24.8 28.7 %all-to-all-start = ((f32[4,2,32,512]{3,2,1,0:T(8,128)}), f32[4,2,32,512]{3,2,1,0:T(8,128)S(1)}, u32[]{:S(2)}, u32[]{:S(2)}) async-start(f32[4,2,32,512]{3,2,1,0:T(8,128)} %broadcast_in_dim.180), calls=%async_computation | async-start | bytes 1048576 | tf_op jit(solution)/shard_map/all_to_all | solution.py:73
  36.3 17.2 %collective-permute-start.2 = (f32[32,768]{1,0:T(8,128)S(1)}, f32[32,768]{1,0:T(8,128)S(1)}, u32[]{:S(2)}, u32[]{:S(2)}) collective-permute-start(f32[32,768]{1,0:T(8,128)S(1)} %collective-permute-done.1), channel_id=1, source_target_pairs={{0,0},{8,56},{16,48},{24,40},{32,32},{40,24},{48,16},{56,8},{64,72... | collective-permute-start | bytes 294920 | tf_op jit(solution)/shard_map/ppermute | solution.py:63
  53.5 8.7 %collective-permute-start.3 = (f32[384,512]{1,0:T(8,128)S(1)}, f32[384,512]{1,0:T(8,128)S(1)}, u32[]{:S(2)}, u32[]{:S(2)}) collective-permute-start(f32[384,512]{1,0:T(8,128)S(1)} %all-gather), channel_id=1, source_target_pairs={{0,1},{1,0},{2,3},{3,2},{4,5},{5,4},{6,7},{7,6},{8,9},{9,8},{10,11... | collective-permute-start | bytes 2359304 | tf_op jit(solution)/shard_map/ppermute | solution.py:50
  91.8 25.9 %all-to-all-start.2 = ((f32[8,32,768]{2,1,0:T(8,128)}), f32[8,32,768]{2,1,0:T(8,128)S(1)}, u32[]{:S(2)}, u32[]{:S(2)}) async-start(f32[8,32,768]{2,1,0:T(8,128)} %broadcast_in_dim.189), calls=%async_computation.2 | async-start | bytes 1572864 | tf_op jit(solution)/shard_map/all_to_all | solution.py:129
  119.0 15.0 %all-to-all-start.3 = ((f32[8,32,256]{2,1,0:T(8,128)}), f32[8,32,256]{2,1,0:T(8,128)S(1)}, u32[]{:S(2)}, u32[]{:S(2)}) async-start(f32[8,32,256]{2,1,0:T(8,128)} %fusion.39), calls=%async_computation.3 | async-start | bytes 524288 | tf_op jit(solution)/shard_map/all_to_all | solution.py:54
  123.8 10.1 %copy-start = (f32[256,32]{0,1:T(8,128)S(1)}, f32[256,32]{0,1:T(8,128)}, u32[]{:S(2)}) copy-start(f32[256,32]{0,1:T(8,128)} %param.9) | copy-start | bytes 98308
  137.5 13.2 %all-to-all-start.4 = ((f32[8,2,32,128]{3,1,2,0:T(2,128)}), f32[8,2,32,128]{3,1,2,0:T(2,128)S(1)}, u32[]{:S(2)}, u32[]{:S(2)}) async-start(f32[8,2,32,128]{3,1,2,0:T(2,128)} %bitcast.73), calls=%async_computation.4 | async-start | bytes 524288 | tf_op jit(solution)/shard_map/all_to_all | solution.py:54
  150.7 29.9 %copy-start.2 = (f32[2,128,16]{1,2,0:T(8,128)S(1)}, f32[2,128,16]{1,2,0:T(8,128)}, u32[]{:S(2)}) copy-start(f32[2,128,16]{1,2,0:T(8,128)} %param.12) | copy-start | bytes 49156
  151.4 8.1 %all-to-all-start.5 = ((f32[4,2,32,128]{3,2,1,0:T(8,128)}), f32[4,2,32,128]{3,2,1,0:T(8,128)S(1)}, u32[]{:S(2)}, u32[]{:S(2)}) async-start(f32[4,2,32,128]{3,2,1,0:T(8,128)} %broadcast_in_dim.190), calls=%async_computation.5 | async-start | bytes 262144 | tf_op jit(solution)/shard_map/all_to_all | solution.py:73
  167.8 12.8 %all-to-all-start.6 = ((f32[8,2,16,128]{3,2,1,0:T(8,128)}), f32[8,2,16,128]{3,2,1,0:T(8,128)S(1)}, u32[]{:S(2)}, u32[]{:S(2)}) async-start(f32[8,2,16,128]{3,2,1,0:T(8,128)} %copy.25), calls=%async_computation.6 | async-start | bytes 262144 | tf_op jit(solution)/shard_map/all_to_all | solution.py:54
Sparse Core Ops, SparseCore 0:
  23.6 85.1 all-gather.5
